TPU v7x, 32 devices: a whole 2x2x4 slice. The times are simulated.
32 devices in a mesh: shell: 16 (over z, y, x), sky: 2 (over core).
Axes of the slice: x: 2, y: 2, z: 4, core: 2. Of those that a mesh axis runs over, the one named last changes fastest.
Arguments:
- excitation: float32 [512, 65536], P('shell', 'sky'), may hold values from -1.8 to 1.8
- star_shell: int32 [32, 32, 128], P(('shell', 'sky')), may hold values from 0 to 31
- star_pixel: int32 [32, 32, 128], P(('shell', 'sky')), may hold values from 0 to 32767
- star_fraction: float32 [32, 32, 128], P(('shell', 'sky')), may hold values from 0 to 1
- star_count: int32 [32, 32], P(('shell', 'sky')), may hold values from 0 to 128, as said below
- observed: float32 [32, 32, 128], P(None, ('shell', 'sky')), may hold values from 0 to 1
- inverse_error: float32 [32, 32, 128], P(None, ('shell', 'sky')), may hold values from 1 to 8
Outputs:
- extinction: float32 [512, 65536], P('shell', 'sky')
- sensitivity: float32 [512, 65536], P('shell', 'sky')
- residual: float32 [32, 32, 128], P(None, ('shell', 'sky'))
Inputs may be any that keep to these rules, and one draw needn't show every extreme that they name: `star_count`: live slots from holder h to owner o. In every draw some owner gets 128 live slots from every holder; holders' loads differ.
All inputs are finite; a program needn't handle non-finite values.
Results may differ from a plain program's by a relative error of at most 0.00018.
Values sent between devices are 32-bit elements; how exact they have to be, the bound alone decides.
A program may use at most 128 MiB of HBM per device.

v0:
```python
import jax
import jax.numpy as jnp
from jax import lax
from jax.sharding import PartitionSpec as P

PASSES = 4


depth_span = 2.0


def padded_2(shard, sides, width):
    for axis, dim in sides:
        size, length = (lax.axis_size(axis), shard.shape[dim])
        up = [(i, (i + 1) % size) for i in range(size - 1)]
        down = [(j, i) for i, j in up]
        last = lax.slice_in_dim(shard, length - width, length, axis=dim)
        leading = lax.slice_in_dim(shard, 0, width, axis=dim)
        before = lax.ppermute(last, axis, up)
        after = lax.ppermute(leading, axis, down)
        shard = jnp.concatenate([before, shard, after], axis=dim)
    return shard


def body(excitation, star_shell, star_pixel, star_fraction, star_count, observed, inverse_error):
    shell_rows = excitation.shape[0]
    pixel_cols = excitation.shape[1]
    shell_devices = lax.axis_size("shell")
    shells_all = shell_rows * shell_devices
    thickness = depth_span / shells_all
    logdens = excitation
    for sweep in range(PASSES):
        padded = padded_2(logdens, (("shell", 0),), 1)
        logdens = 0.3 * (padded[:-2] + padded[2:]) + 0.35 * logdens + excitation
    density = jnp.exp(logdens)
    row_ids = jnp.arange(shell_rows, dtype=jnp.int32)
    lower_ones = (row_ids[:, None] >= row_ids[None, :]).astype(jnp.float32)
    upper_ones = (row_ids[:, None] <= row_ids[None, :]).astype(jnp.float32)
    local_prefix = jnp.dot(
        lower_ones,
        density * thickness,
        precision=lax.Precision.HIGHEST,
        preferred_element_type=jnp.float32,
    )
    block_ids = jnp.arange(shell_devices, dtype=jnp.int32)
    strict_lower = (block_ids[:, None] > block_ids[None, :]).astype(jnp.float32)
    strict_upper = (block_ids[:, None] < block_ids[None, :]).astype(jnp.float32)
    slice_width = pixel_cols // shell_devices
    spread = local_prefix[-1].reshape(shell_devices, slice_width)
    summed = jnp.dot(
        strict_lower,
        lax.all_to_all(spread, "shell", split_axis=0, concat_axis=0, tiled=True),
        precision=lax.Precision.HIGHEST,
        preferred_element_type=jnp.float32,
    )
    offset = lax.all_to_all(summed, "shell", split_axis=0, concat_axis=0, tiled=True).reshape(-1)
    extinction = local_prefix + offset[None, :]
    slot_shape = star_shell.shape
    cell_count = shell_rows * pixel_cols
    flat_cell = (star_shell * pixel_cols + star_pixel).reshape(-1)
    ext_at = jnp.take(extinction.reshape(-1), flat_cell).reshape(slot_shape)
    dens_at = jnp.take(density.reshape(-1), flat_cell).reshape(slot_shape)
    slot_alive = (
        jnp.arange(slot_shape[2], dtype=jnp.int32)[None, None, :] < star_count[:, :, None]
    ).astype(jnp.int32)
    near_share = 1.0 - star_fraction
    looked = ext_at - near_share * thickness * dens_at
    column = jnp.where(slot_alive > 0, looked, 0.0)
    owner_column, owner_alive = (
        lax.all_to_all(column, ("shell", "sky"), split_axis=1, concat_axis=0, tiled=True),
        lax.all_to_all(slot_alive, ("shell", "sky"), split_axis=1, concat_axis=0, tiled=True),
    )
    transmit = jnp.exp(-owner_column)
    residual = jnp.where(owner_alive > 0, (observed - (1.0 - transmit)) * inverse_error, 0.0)
    pull_back = -residual * inverse_error * transmit
    returned = lax.all_to_all(pull_back, ("shell", "sky"), split_axis=0, concat_axis=1, tiled=True)
    both_index = jnp.concatenate((flat_cell, flat_cell + cell_count), 0)
    both_values = jnp.concatenate((returned.reshape(-1), (near_share * returned).reshape(-1)), 0)
    accumulated = (
        jnp.zeros((2 * cell_count,), jnp.float32)
        .at[both_index]
        .add(both_values)
        .reshape(2, shell_rows, pixel_cols)
    )
    impulse = accumulated[0]
    nearby = accumulated[1]
    local_suffix = jnp.dot(
        upper_ones, impulse, precision=lax.Precision.HIGHEST, preferred_element_type=jnp.float32
    )
    spread_tails = local_suffix[0].reshape(shell_devices, slice_width)
    summed = jnp.dot(
        strict_upper,
        lax.all_to_all(spread_tails, "shell", split_axis=0, concat_axis=0, tiled=True),
        precision=lax.Precision.HIGHEST,
        preferred_element_type=jnp.float32,
    )
    tail_offset = lax.all_to_all(summed, "shell", split_axis=0, concat_axis=0, tiled=True).reshape(
        -1
    )
    sensitivity = density * (local_suffix + tail_offset[None, :] - nearby)
    return (extinction, sensitivity, residual)


def solution(mesh):
    placed = (
        P("shell", "sky"),
        P(("shell", "sky"), None, None),
        P(("shell", "sky"), None, None),
        P(("shell", "sky"), None, None),
        P(("shell", "sky"), None),
        P(None, ("shell", "sky"), None),
        P(None, ("shell", "sky"), None),
    )
    return jax.shard_map(
        body,
        mesh=mesh,
        in_specs=placed,
        out_specs=(P("shell", "sky"), P("shell", "sky"), P(None, ("shell", "sky"), None)),
        check_vma=False,
    )
```

profile of v0, /device:TPU:0, one launch (start us, length us, event | category | flops | bytes accessed | tf_op | source)
XLA Modules:
  0.0 324.0 jit_solution(10690383520463945199)
XLA Ops:
  2.4 4.8 %collective-permute-start = (f32[1,32768]{1,0:T(1,128)S(1)}, f32[1,32768]{1,0:T(1,128)S(1)}, u32[]{:S(2)}, u32[]{:S(2)}) collective-permute-start(f32[1,32768]{1,0:T(1,128)S(1)} %get-tuple-element.25), channel_id=1, source_target_pairs={{0,2},{2,4},{4,6},{6,8},{8,10},{10,12},{12,14},{14,16},{16,18},{18... | collective-permute-start | bytes 393224 | tf_op jit(solution)/shard_map/ppermute | solution.py:19
  9.9 4.8 %collective-permute-done.1 = f32[1,32768]{1,0:T(1,128)S(1)} collective-permute-done((f32[1,32768]{1,0:T(1,128)S(1)}, f32[1,32768]{1,0:T(1,128)S(1)}, u32[]{:S(2)}, u32[]{:S(2)}) %collective-permute-start.1) | collective-permute-done | bytes 131104 | tf_op jit(solution)/shard_map/ppermute | solution.py:20
  14.7 5.7 %fusion.16 = f32[32,32768]{1,0:T(8,128)S(1)} fusion(f32[32,32768]{1,0:T(8,128)} %param.9, f32[1,32768]{1,0:T(1,128)S(1)} %collective-permute-done.1, f32[1,32768]{1,0:T(1,128)S(1)} %collective-permute-done), kind=kLoop, calls=%fused_computation.26 | loop fusion | flops 7340032 | bytes 8650752 | tf_op jit(solution)/shard_map/add | solution.py:34
  20.6 4.0 %collective-permute-start.2 = (f32[1,32768]{1,0:T(1,128)S(1)}, f32[1,32768]{1,0:T(1,128)S(1)}, u32[]{:S(2)}, u32[]{:S(2)}) collective-permute-start(f32[1,32768]{1,0:T(1,128)S(1)} %get-tuple-element.23), channel_id=1, source_target_pairs={{0,2},{2,4},{4,6},{6,8},{8,10},{10,12},{12,14},{14,16},{16,18},{18... | collective-permute-start | bytes 393224 | tf_op jit(solution)/shard_map/ppermute | solution.py:19
  27.1 4.4 %collective-permute-done.3 = f32[1,32768]{1,0:T(1,128)S(1)} collective-permute-done((f32[1,32768]{1,0:T(1,128)S(1)}, f32[1,32768]{1,0:T(1,128)S(1)}, u32[]{:S(2)}, u32[]{:S(2)}) %collective-permute-start.3) | collective-permute-done | bytes 131104 | tf_op jit(solution)/shard_map/ppermute | solution.py:20
  33.2 4.0 %collective-permute-start.4 = (f32[1,32768]{1,0:T(1,128)S(1)}, f32[1,32768]{1,0:T(1,128)S(1)}, u32[]{:S(2)}, u32[]{:S(2)}) collective-permute-start(f32[1,32768]{1,0:T(1,128)S(1)} %get-tuple-element.21), channel_id=1, source_target_pairs={{0,2},{2,4},{4,6},{6,8},{8,10},{10,12},{12,14},{14,16},{16,18},{18... | collective-permute-start | bytes 393224 | tf_op jit(solution)/shard_map/ppermute | solution.py:19
  39.7 4.4 %collective-permute-done.5 = f32[1,32768]{1,0:T(1,128)S(1)} collective-permute-done((f32[1,32768]{1,0:T(1,128)S(1)}, f32[1,32768]{1,0:T(1,128)S(1)}, u32[]{:S(2)}, u32[]{:S(2)}) %collective-permute-start.5) | collective-permute-done | bytes 131104 | tf_op jit(solution)/shard_map/ppermute | solution.py:20
  45.8 4.6 %collective-permute-start.6 = (f32[1,32768]{1,0:T(1,128)S(1)}, f32[1,32768]{1,0:T(1,128)S(1)}, u32[]{:S(2)}, u32[]{:S(2)}) collective-permute-start(f32[1,32768]{1,0:T(1,128)S(1)} %get-tuple-element.19), channel_id=1, source_target_pairs={{0,2},{2,4},{4,6},{6,8},{8,10},{10,12},{12,14},{14,16},{16,18},{18... | collective-permute-start | bytes 393224 | tf_op jit(solution)/shard_map/ppermute | solution.py:19
  63.5 13.8 %all_to_all.72 = f32[16,1,2048]{2,1,0:T(1,128)S(1)} all-to-all(f32[16,1,2048]{2,1,0:T(1,128)S(1)} %bitcast.77), channel_id=1, replica_groups=mesh['shell'=16,'sky'=2] {'shell'}, dimensions={0} | all-to-all | bytes 262144 | tf_op jit(solution)/shard_map/all_to_all | solution.py:52
  82.5 4.9 %copy.59 = f32[4,256,8,128]{3,1,2,0:T(8,128)} copy(f32[4,256,8,128]{3,2,1,0:T(8,128)} %bitcast.73) | data formatting | bytes 8388608
  87.4 52.1 %gather_fusion.1 = f32[4096]{0:T(1024)S(1)} fusion(f32[1048576]{0:T(1024)} %bitcast.72, s32[4096]{0:T(1024)S(1)} %get-tuple-element.15), kind=kCustom, calls=%fused_computation.1.clone | custom fusion | bytes 49152 | tf_op jit(solution)/shard_map/jit(_take)/gather | solution.py:62
  139.5 5.9 %all-to-all-start.2 = ((s32[1,32,128]{2,0,1:T(1,128)}), s32[1,32,128]{2,0,1:T(1,128)S(1)}, u32[]{:S(2)}, u32[]{:S(2)}) async-start(s32[1,32,128]{2,0,1:T(1,128)} %bitcast.8), calls=%async_computation.2 | async-start | bytes 32768 | tf_op jit(solution)/shard_map/all_to_all | solution.py:71
  150.6 52.1 %gather_fusion = f32[4096]{0:T(1024)S(1)} fusion(f32[1048576]{0:T(1024)} %bitcast.71, s32[4096]{0:T(1024)S(1)} %get-tuple-element.15), kind=kCustom, calls=%fused_computation.clone | custom fusion | bytes 49152 | tf_op jit(solution)/shard_map/jit(_take)/gather | solution.py:61
  203.4 5.8 %all-to-all-start.3 = ((f32[1,32,128]{2,0,1:T(1,128)}), f32[1,32,128]{2,0,1:T(1,128)S(1)}, u32[]{:S(2)}, u32[]{:S(2)}) async-start(f32[1,32,128]{2,0,1:T(1,128)} %bitcast.14), calls=%async_computation.3 | async-start | bytes 32768 | tf_op jit(solution)/shard_map/all_to_all | solution.py:70
  209.3 7.1 %all-to-all-done.3 = f32[1,32,128]{2,0,1:T(1,128)S(1)} async-done(((f32[1,32,128]{2,0,1:T(1,128)}), f32[1,32,128]{2,0,1:T(1,128)S(1)}, u32[]{:S(2)}, u32[]{:S(2)}) %all-to-all-start.3) | async-done | bytes 16416 | tf_op jit(solution)/shard_map/all_to_all | solution.py:70
  219.7 6.8 %all-to-all-done.4 = f32[32,1,128]{2,1,0:T(1,128)S(1)} async-done(((f32[32,1,128]{2,1,0:T(1,128)}), f32[32,1,128]{2,1,0:T(1,128)S(1)}, u32[]{:S(2)}, u32[]{:S(2)}) %all-to-all-start.4) | async-done | bytes 16416 | tf_op jit(solution)/shard_map/all_to_all | solution.py:76
  226.6 47.0 %scatter_custom_fusion = f32[2097152]{0:T(1024)} fusion(s32[8192]{0:T(1024)S(1)} %bitcast.85, f32[8192]{0:T(1024)S(1)} %pad_maximum_fusion.8, f32[]{:T(128)} %constant.0.clone.1), kind=kCustom, calls=%fused_computation.29 | custom fusion | flops 8192 | bytes 8388612 | tf_op jit(solution)/shard_map/scatter-add | solution.py:82
  273.6 7.3 %fusion.36 = (f32[1048576]{0:T(1024)}, f32[1048576]{0:T(1024)}) fusion(f32[2097152]{0:T(1024)} %scatter_custom_fusion), kind=kLoop, calls=%fused_computation.66 | loop fusion | bytes 16777216 | tf_op jit(solution)/shard_map/slice | solution.py:85
  280.9 4.9 %slice.108 = f32[32,32768]{1,0:T(8,128)} reshape(f32[1048576]{0:T(1024)} %get-tuple-element.17) | data formatting | bytes 8388608 | tf_op jit(solution)/shard_map/slice | solution.py:85
  285.8 4.4 %fusion.32 = f32[32,32768]{1,0:T(8,128)S(1)} fusion(f32[32,32768]{1,0:T(8,128)} %slice.108), kind=kOutput, calls=%fused_computation.60 | convolution fusion | flops 402654208 | bytes 8388608 | tf_op jit(solution)/shard_map/dot_general | solution.py:87
  292.3 10.4 %all_to_all.73 = f32[16,1,2048]{2,1,0:T(1,128)S(1)} all-to-all(f32[16,1,2048]{2,1,0:T(1,128)S(1)} %bitcast.78), channel_id=1, replica_groups=mesh['shell'=16,'sky'=2] {'shell'}, dimensions={0} | all-to-all | bytes 262144 | tf_op jit(solution)/shard_map/all_to_all | solution.py:93
  307.2 4.5 %broadcast_add_fusion = f32[32,32768]{1,0:T(8,128)} fusion(f32[32,32768]{1,0:T(8,128)} %copy-done.2, f32[32768]{0:T(1024)S(1)} %bitcast.75), kind=kLoop, calls=%fused_computation.35 | loop fusion | flops 1048576 | bytes 8519680 | tf_op jit(solution)/shard_map/add | solution.py:57
  311.8 4.9 %slice.111 = f32[32,32768]{1,0:T(8,128)} reshape(f32[1048576]{0:T(1024)} %get-tuple-element.18) | data formatting | bytes 8388608 | tf_op jit(solution)/shard_map/slice | solution.py:86
  316.7 7.3 %subtract_multiply_fusion = f32[32,32768]{1,0:T(8,128)} fusion(f32[32,32768]{1,0:T(8,128)} %copy-done.1, f32[32,32768]{1,0:T(8,128)} %slice.111, f32[32,32768]{1,0:T(8,128)} %copy-done.3, f32[32768]{0:T(1024)S(1)} %bitcast.76), kind=kLoop, calls=%fused_computation.28 | loop fusion | flops 3145728 | bytes 16908288 | tf_op jit(solution)/shard_map/mul | solution.py:100
  (59 shorter events, 47.2 us)
Async XLA Ops:
  2.4 7.6 %collective-permute-start = (f32[1,32768]{1,0:T(1,128)S(1)}, f32[1,32768]{1,0:T(1,128)S(1)}, u32[]{:S(2)}, u32[]{:S(2)}) collective-permute-start(f32[1,32768]{1,0:T(1,128)S(1)} %get-tuple-element.25), channel_id=1, source_target_pairs={{0,2},{2,4},{4,6},{6,8},{8,10},{10,12},{12,14},{14,16},{16,18},{18... | collective-permute-start | bytes 393224 | tf_op jit(solution)/shard_map/ppermute | solution.py:19
  7.2 24.2 %copy-start = (f32[32,32768]{1,0:T(8,128)S(1)}, f32[32,32768]{1,0:T(8,128)}, u32[]{:S(2)}) copy-start(f32[32,32768]{1,0:T(8,128)} %param.9) | copy-start | bytes 12582916
  7.2 7.5 %collective-permute-start.1 = (f32[1,32768]{1,0:T(1,128)S(1)}, f32[1,32768]{1,0:T(1,128)S(1)}, u32[]{:S(2)}, u32[]{:S(2)}) collective-permute-start(f32[1,32768]{1,0:T(1,128)S(1)} %get-tuple-element.26), channel_id=1, source_target_pairs={{2,0},{4,2},{6,4},{8,6},{10,8},{12,10},{14,12},{16,14},{18,16},{20... | collective-permute-start | bytes 393224 | tf_op jit(solution)/shard_map/ppermute | solution.py:20
  20.6 6.5 %collective-permute-start.2 = (f32[1,32768]{1,0:T(1,128)S(1)}, f32[1,32768]{1,0:T(1,128)S(1)}, u32[]{:S(2)}, u32[]{:S(2)}) collective-permute-start(f32[1,32768]{1,0:T(1,128)S(1)} %get-tuple-element.23), channel_id=1, source_target_pairs={{0,2},{2,4},{4,6},{6,8},{8,10},{10,12},{12,14},{14,16},{16,18},{18... | collective-permute-start | bytes 393224 | tf_op jit(solution)/shard_map/ppermute | solution.py:19
  24.6 6.9 %collective-permute-start.3 = (f32[1,32768]{1,0:T(1,128)S(1)}, f32[1,32768]{1,0:T(1,128)S(1)}, u32[]{:S(2)}, u32[]{:S(2)}) collective-permute-start(f32[1,32768]{1,0:T(1,128)S(1)} %get-tuple-element.24), channel_id=1, source_target_pairs={{2,0},{4,2},{6,4},{8,6},{10,8},{12,10},{14,12},{16,14},{18,16},{20... | collective-permute-start | bytes 393224 | tf_op jit(solution)/shard_map/ppermute | solution.py:20
  33.2 6.5 %collective-permute-start.4 = (f32[1,32768]{1,0:T(1,128)S(1)}, f32[1,32768]{1,0:T(1,128)S(1)}, u32[]{:S(2)}, u32[]{:S(2)}) collective-permute-start(f32[1,32768]{1,0:T(1,128)S(1)} %get-tuple-element.21), channel_id=1, source_target_pairs={{0,2},{2,4},{4,6},{6,8},{8,10},{10,12},{12,14},{14,16},{16,18},{18... | collective-permute-start | bytes 393224 | tf_op jit(solution)/shard_map/ppermute | solution.py:19
  37.2 6.9 %collective-permute-start.5 = (f32[1,32768]{1,0:T(1,128)S(1)}, f32[1,32768]{1,0:T(1,128)S(1)}, u32[]{:S(2)}, u32[]{:S(2)}) collective-permute-start(f32[1,32768]{1,0:T(1,128)S(1)} %get-tuple-element.22), channel_id=1, source_target_pairs={{2,0},{4,2},{6,4},{8,6},{10,8},{12,10},{14,12},{16,14},{18,16},{20... | collective-permute-start | bytes 393224 | tf_op jit(solution)/shard_map/ppermute | solution.py:20
  45.8 8.4 %collective-permute-start.6 = (f32[1,32768]{1,0:T(1,128)S(1)}, f32[1,32768]{1,0:T(1,128)S(1)}, u32[]{:S(2)}, u32[]{:S(2)}) collective-permute-start(f32[1,32768]{1,0:T(1,128)S(1)} %get-tuple-element.19), channel_id=1, source_target_pairs={{0,2},{2,4},{4,6},{6,8},{8,10},{10,12},{12,14},{14,16},{16,18},{18... | collective-permute-start | bytes 393224 | tf_op jit(solution)/shard_map/ppermute | solution.py:19
  50.4 6.9 %collective-permute-start.7 = (f32[1,32768]{1,0:T(1,128)S(1)}, f32[1,32768]{1,0:T(1,128)S(1)}, u32[]{:S(2)}, u32[]{:S(2)}) collective-permute-start(f32[1,32768]{1,0:T(1,128)S(1)} %get-tuple-element.20), channel_id=1, source_target_pairs={{2,0},{4,2},{6,4},{8,6},{10,8},{12,10},{14,12},{16,14},{18,16},{20... | collective-permute-start | bytes 393224 | tf_op jit(solution)/shard_map/ppermute | solution.py:20
  59.1 2.5 copy-start.1
  59.1 22.6 %copy-start.9 = (s32[1,32]{1,0:T(1,128)S(1)}, s32[1,32]{1,0:T(1,128)}, u32[]{:S(2)}) copy-start(s32[1,32]{1,0:T(1,128)} %param.13) | copy-start | bytes 388
  59.1 23.3 %copy-start.5 = (s32[1,32,128]{2,1,0:T(8,128)S(1)}, s32[1,32,128]{2,1,0:T(8,128)}, u32[]{:S(2)}) copy-start(s32[1,32,128]{2,1,0:T(8,128)} %param.11) | copy-start | bytes 49156
  59.1 23.3 %copy-start.6 = (s32[1,32,128]{2,1,0:T(8,128)S(1)}, s32[1,32,128]{2,1,0:T(8,128)}, u32[]{:S(2)}) copy-start(s32[1,32,128]{2,1,0:T(8,128)} %param.10) | copy-start | bytes 49156
  61.5 2.0 copy-start.2
  78.2 61.3 %all-to-all-start.1 = ((f32[16,1,2048]{2,1,0:T(1,128)}), f32[16,1,2048]{2,1,0:T(1,128)S(1)}, u32[]{:S(2)}, u32[]{:S(2)}) async-start(f32[16,1,2048]{2,1,0:T(1,128)} %copy.44), calls=%async_computation.1 | async-start | bytes 262144 | tf_op jit(solution)/shard_map/all_to_all | solution.py:56
  139.5 63.9 %all-to-all-start.2 = ((s32[1,32,128]{2,0,1:T(1,128)}), s32[1,32,128]{2,0,1:T(1,128)S(1)}, u32[]{:S(2)}, u32[]{:S(2)}) async-start(s32[1,32,128]{2,0,1:T(1,128)} %bitcast.8), calls=%async_computation.2 | async-start | bytes 32768 | tf_op jit(solution)/shard_map/all_to_all | solution.py:71
  150.6 52.1 %copy-start.4 = (f32[1,32,128]{2,1,0:T(8,128)S(1)}, f32[1,32,128]{2,1,0:T(8,128)}, u32[]{:S(2)}) copy-start(f32[1,32,128]{2,1,0:T(8,128)} %param.12) | copy-start | bytes 49156
  150.6 65.7 %copy-start.7 = (f32[32,1,128]{2,1,0:T(1,128)S(1)}, f32[32,1,128]{2,1,0:T(1,128)}, u32[]{:S(2)}) copy-start(f32[32,1,128]{2,1,0:T(1,128)} %param.15) | copy-start | bytes 49156
  150.6 65.7 %copy-start.8 = (f32[32,1,128]{2,1,0:T(1,128)S(1)}, f32[32,1,128]{2,1,0:T(1,128)}, u32[]{:S(2)}) copy-start(f32[32,1,128]{2,1,0:T(1,128)} %param.14) | copy-start | bytes 49156
  203.4 12.9 %all-to-all-start.3 = ((f32[1,32,128]{2,0,1:T(1,128)}), f32[1,32,128]{2,0,1:T(1,128)S(1)}, u32[]{:S(2)}, u32[]{:S(2)}) async-start(f32[1,32,128]{2,0,1:T(1,128)} %bitcast.14), calls=%async_computation.3 | async-start | bytes 32768 | tf_op jit(solution)/shard_map/all_to_all | solution.py:70
  217.0 9.6 %all-to-all-start.4 = ((f32[32,1,128]{2,1,0:T(1,128)}), f32[32,1,128]{2,1,0:T(1,128)S(1)}, u32[]{:S(2)}, u32[]{:S(2)}) async-start(f32[32,1,128]{2,1,0:T(1,128)} %bitcast.19), calls=%async_computation.4 | async-start | bytes 32768 | tf_op jit(solution)/shard_map/all_to_all | solution.py:76
  290.3 2.0 copy-start.3
  303.7 13.0 %all-to-all-start.6 = ((f32[16,1,2048]{2,1,0:T(1,128)}), f32[16,1,2048]{2,1,0:T(1,128)S(1)}, u32[]{:S(2)}, u32[]{:S(2)}) async-start(f32[16,1,2048]{2,1,0:T(1,128)} %copy.54), calls=%async_computation.6 | async-start | bytes 262144 | tf_op jit(solution)/shard_map/all_to_all | solution.py:97
where the time goes:
time: 328 us; the launch traced here: 324 us
  local copies, waits for them, and re-layouts  137 us (42%)
  other arithmetic  74 us (23%)
  starting transfers between devices  44.3 us (14%)
  waiting for transfers between devices  36.5 us (11%)
  blocking collectives  24.1 us (7%)
  matrix products  7.15 us (2%)
    gather x1, local copies, waits for them, and re-layouts, body(): dens_at = jnp.take(density.reshape(-1), flat_cell).reshape(slot_shape)  52.1 us
    gather x1, local copies, waits for them, and re-layouts, body(): ext_at = jnp.take(extinction.reshape(-1), flat_cell).reshape(slot_shape)  52.1 us
    scatter-add x1, other arithmetic, body(): accumulated = jnp.zeros((2 * cell_count,), jnp.float32).at[both_index].ad...  47 us
    ppermute x4, starting transfers between devices, padded_2(): before = lax.ppermute(last, axis, up)  17.4 us
    ppermute x4, waiting for transfers between devices, padded_2(): after = lax.ppermute(leading, axis, down)  16.5 us
    all_to_all x1, blocking collectives, body(): lax.all_to_all(spread, 'shell', split_axis=0, concat_axis=0, tiled=True)  13.8 us
    slice x2, local copies, waits for them, and re-layouts, body(): impulse = accumulated[0]  12.3 us
    unnamed x22, local copies, waits for them, and re-layouts  11.6 us
  transfers between devices with their start and end apart: 13, of which 10 were waited for; matrix products, arithmetic and copies ran while one was open for 39% of the time, Pallas kernels for 0%

commit v1 on v0

v1 whole, which is shorter than its diff:
```python
import jax
import jax.numpy as jnp
import numpy as np
from jax import lax
from jax.experimental import pallas as pl
from jax.experimental.pallas import tpu as pltpu
from jax.sharding import PartitionSpec as P

PASSES = 4
LANES = 128
TILE = 2048

depth_span = 2.0


def split2(x):
    high = x.astype(jnp.bfloat16).astype(jnp.float32)
    return high, x - high


def stencil_matrix(rows, first, last):
    wide = rows + 2 * PASSES
    valid = np.ones((wide, 1))
    if first:
        valid[:PASSES] = 0.0
    if last:
        valid[-PASSES:] = 0.0
    eye = np.eye(wide)
    out = eye
    for _ in range(PASSES):
        padded = np.pad(out, ((1, 1), (0, 0)))
        out = valid * (0.3 * (padded[:-2] + padded[2:]) + 0.35 * out + eye)
    out = out[PASSES:-PASSES]
    local = out[:, PASSES:-PASSES]
    halo = np.concatenate([out[:, :PASSES], out[:, -PASSES:]], 1)
    return np.concatenate([local, local, halo, halo], 1).astype(np.float32)


def density_kernel(
    n_own, thickness, row_ref, lo_ref, mat_ref, tri_ref, exc_ref, bef_ref, aft_ref,
    dens_ref, pre_ref, sum_ref, base_ref, slope_ref, pre_tab, dens_tab, got,
):
    step = pl.program_id(0)
    rows, width = exc_ref.shape
    blocks = width // LANES
    e1, e2 = split2(exc_ref[...])
    h1, h2 = split2(jnp.concatenate([bef_ref[...], aft_ref[...]], 0))
    stacked = jnp.concatenate([e1, e2, h1, h2], 0).astype(jnp.bfloat16)
    both = jnp.dot(mat_ref[...], stacked, preferred_element_type=jnp.float32)
    dens = jnp.exp(both[:rows] + both[rows:])
    d1, d2 = split2(dens)
    pre = thickness * jnp.dot(
        tri_ref[...],
        jnp.concatenate([d1, d2], 0).astype(jnp.bfloat16),
        preferred_element_type=jnp.float32,
    )
    dens_ref[...] = dens
    pre_ref[...] = pre
    sum_ref[...] = pre[rows - 1 : rows]
    for b in range(blocks):
        at = pl.ds(pl.multiple_of((step * blocks + b) * rows, rows), rows)
        pre_tab[at, :] = pre[:, b * LANES : (b + 1) * LANES]
        dens_tab[at, :] = dens[:, b * LANES : (b + 1) * LANES]

    @pl.when(step == pl.num_programs(0) - 1)
    def _():
        lane = lax.broadcasted_iota(jnp.int32, (LANES, LANES), 1)
        sub = lax.broadcasted_iota(jnp.int32, (LANES, LANES), 0)

        def chunk(pair, carry):
            for k in range(2):
                o = pair * 2 + k
                for c in range(LANES):
                    at = row_ref[o, c]
                    got[k, c : c + 1, :] = pre_tab[pl.ds(at, 1), :]
                    got[k, LANES + c : LANES + c + 1, :] = dens_tab[pl.ds(at, 1), :]
            for k in range(2):
                o = pair * 2 + k
                hot = (sub == lo_ref[pl.ds(o, 1), :]).astype(jnp.bfloat16)
                g1, g2 = split2(got[k])
                picked = jnp.dot(
                    jnp.concatenate([g1, g2], 0).astype(jnp.bfloat16),
                    hot,
                    preferred_element_type=jnp.float32,
                )
                p = picked[:LANES] + picked[2 * LANES : 3 * LANES]
                d = picked[LANES : 2 * LANES] + picked[3 * LANES :]
                base_ref[pl.ds(o, 1), :] = jnp.sum(jnp.where(sub == lane, p, 0.0), 0, keepdims=True)
                slope_ref[pl.ds(o, 1), :] = jnp.sum(jnp.where(sub == lane, d, 0.0), 0, keepdims=True)
            return carry

        lax.fori_loop(0, n_own // 2, chunk, 0)


def column_kernel(n_own, thickness, hi_ref, lo_ref, share_ref, live_ref, base_ref, slope_ref, off_ref, col_ref):
    groups = off_ref.shape[0]
    o1, o2 = split2(off_ref[...])
    table = jnp.concatenate([o1.T, o2.T], 0).astype(jnp.bfloat16)
    tall = lax.broadcasted_iota(jnp.int32, (groups, LANES), 0)
    sub = lax.broadcasted_iota(jnp.int32, (LANES, LANES), 0)

    def chunk(o, carry):
        hot = (tall == hi_ref[pl.ds(o, 1), :]).astype(jnp.bfloat16)
        got = jnp.dot(table, hot, preferred_element_type=jnp.float32)
        got = got[:LANES] + got[LANES:]
        off = jnp.sum(jnp.where(sub == lo_ref[pl.ds(o, 1), :], got, 0.0), 0, keepdims=True)
        at = pl.ds(o, 1)
        col = base_ref[at, :] + off - share_ref[at, :] * thickness * slope_ref[at, :]
        col_ref[at, :] = jnp.where(live_ref[at, :] > 0, col, -1.0)
        return carry

    lax.fori_loop(0, n_own, chunk, 0)


GROUP = 8


def scatter_kernel(
    n_own, row_ref, rows_ref, lo_ref, share_ref, pull_ref, mat_ref,
    s_ref, tail_ref, imp_tab, near_tab, upd,
):
    step = pl.program_id(0)
    rows, width = s_ref.shape
    blocks = width // LANES

    @pl.when(step == 0)
    def _():
        total = imp_tab.shape[0]

        def clear(i, carry):
            at = pl.ds(pl.multiple_of(i * 256, 256), 256)
            imp_tab[at, :] = jnp.zeros((256, LANES), jnp.float32)
            near_tab[at, :] = jnp.zeros((256, LANES), jnp.float32)
            return carry

        lax.fori_loop(0, total // 256, clear, 0)
        sub = lax.broadcasted_iota(jnp.int32, (LANES, LANES), 0)
        lane = lax.broadcasted_iota(jnp.int32, (LANES, LANES), 1)
        grouped = sub // GROUP == lane // GROUP

        def chunk(o, carry):
            at = pl.ds(o, 1)
            same = jnp.broadcast_to(rows_ref[at, :], (LANES, LANES))
            same = jnp.logical_and(same == same.T, grouped)
            pull = pull_ref[at, :]
            a1, a2 = split2(jnp.where(same, pull, 0.0))
            b1, b2 = split2(jnp.where(same, pull * share_ref[at, :], 0.0))
            hot = (sub == lo_ref[at, :]).astype(jnp.bfloat16)
            out = lax.dot_general(
                jnp.concatenate([a1, a2, b1, b2], 0).astype(jnp.bfloat16),
                hot,
                (((1,), (1,)), ((), ())),
                preferred_element_type=jnp.float32,
            )
            upd[:LANES] = out[:LANES] + out[LANES : 2 * LANES]
            upd[LANES:] = out[2 * LANES : 3 * LANES] + out[3 * LANES :]
            for g in range(LANES // GROUP):
                cs = range(g * GROUP, (g + 1) * GROUP)
                where = [row_ref[o, c] for c in cs]
                imps = [imp_tab[pl.ds(w, 1), :] + upd[c : c + 1, :] for w, c in zip(where, cs)]
                nears = [near_tab[pl.ds(w, 1), :] + upd[LANES + c : LANES + c + 1, :] for w, c in zip(where, cs)]
                for w, a, b in zip(where, imps, nears):
                    imp_tab[pl.ds(w, 1), :] = a
                    near_tab[pl.ds(w, 1), :] = b
            return carry

        lax.fori_loop(0, n_own, chunk, 0)

    def natural(tab):
        parts = []
        for b in range(blocks):
            at = pl.ds(pl.multiple_of((step * blocks + b) * rows, rows), rows)
            parts.append(tab[at, :])
        return jnp.concatenate(parts, 1)

    i1, i2 = split2(natural(imp_tab))
    n1, n2 = split2(natural(near_tab))
    out = jnp.dot(
        mat_ref[...],
        jnp.concatenate([i1, i2, n1, n2], 0).astype(jnp.bfloat16),
        preferred_element_type=jnp.float32,
    )
    s_ref[...] = out[:rows]
    tail_ref[...] = out[rows : rows + 1]


def exchange(blocks, size, upper):
    ids = np.arange(size)
    strict = (ids[:, None] < ids[None, :]) if upper else (ids[:, None] > ids[None, :])
    spread = blocks.reshape(size, -1)
    got = lax.all_to_all(spread, "shell", split_axis=0, concat_axis=0, tiled=True)
    summed = jnp.dot(
        jnp.asarray(strict, jnp.float32), got,
        precision=lax.Precision.HIGHEST, preferred_element_type=jnp.float32,
    )
    return lax.all_to_all(summed, "shell", split_axis=0, concat_axis=0, tiled=True)


def body(excitation, star_shell, star_pixel, star_fraction, star_count, observed, inverse_error):
    rows, cols = excitation.shape
    size = lax.axis_size("shell")
    me = lax.axis_index("shell")
    thickness = depth_span / (rows * size)
    n_own = star_shell.shape[1]
    groups = cols // LANES
    tile = min(TILE, cols)
    f32, bf16 = jnp.float32, jnp.bfloat16

    up = [(i, i + 1) for i in range(size - 1)]
    down = [(i + 1, i) for i in range(size - 1)]
    before = lax.ppermute(excitation[-PASSES:], "shell", up)
    after = lax.ppermute(excitation[:PASSES], "shell", down)

    pixel = star_pixel[0]
    hi, lo = pixel // LANES, pixel % LANES
    row = hi * rows + star_shell[0]
    share = 1.0 - star_fraction[0]
    live = (jnp.arange(LANES, dtype=jnp.int32)[None, :] < star_count[0][:, None]).astype(jnp.int32)

    mats = np.stack([stencil_matrix(rows, a, b) for a, b in ((0, 0), (1, 0), (0, 1), (1, 1))])
    top = mats.astype(bf16)
    rest = (mats - top.astype(np.float32)).astype(bf16)
    which = (me == 0).astype(jnp.int32) + 2 * (me == size - 1).astype(jnp.int32)
    mat = lax.dynamic_index_in_dim(jnp.asarray(np.concatenate([top, rest], 1)), which, 0, False)
    tri = np.tril(np.ones((rows, rows), np.float32))
    tri2 = jnp.asarray(np.concatenate([tri, tri], 1).astype(bf16))

    smem = pl.BlockSpec(memory_space=pltpu.SMEM)
    vmem = pl.BlockSpec(memory_space=pltpu.VMEM)
    full = lambda shape: pl.BlockSpec(shape, lambda i: (0, 0))
    cut = lambda r: pl.BlockSpec((r, tile), lambda i: (0, i))
    stars = jax.ShapeDtypeStruct((n_own, LANES), f32)
    grid_shape = jax.ShapeDtypeStruct((rows, cols), f32)
    line = jax.ShapeDtypeStruct((1, cols), f32)
    limit = pltpu.CompilerParams(vmem_limit_bytes=48 * 2**20)

    density, prefix, sums, base, slope = pl.pallas_call(
        lambda *refs: density_kernel(n_own, thickness, *refs),
        grid=(cols // tile,),
        in_specs=[smem, full((n_own, LANES)), full(mat.shape), full(tri2.shape), cut(rows), cut(PASSES), cut(PASSES)],
        out_specs=[cut(rows), cut(rows), cut(1), full((n_own, LANES)), full((n_own, LANES))],
        out_shape=[grid_shape, grid_shape, line, stars, stars],
        scratch_shapes=[
            pltpu.VMEM((groups * rows, LANES), f32),
            pltpu.VMEM((groups * rows, LANES), f32),
            pltpu.VMEM((2, 2 * LANES, LANES), f32),
        ],
        compiler_params=limit,
        name="density",
    )(row, lo, mat, tri2, excitation, before, after)

    offset = exchange(sums, size, False)

    column = pl.pallas_call(
        lambda *refs: column_kernel(n_own, thickness, *refs),
        in_specs=[vmem] * 7,
        out_specs=vmem,
        out_shape=stars,
        compiler_params=limit,
        name="column",
    )(hi, lo, share, live, base, slope, offset.reshape(groups, LANES))

    both = ("shell", "sky")
    owned = lax.all_to_all(column[None], both, split_axis=1, concat_axis=0, tiled=True)
    transmit = jnp.exp(-owned)
    residual = jnp.where(owned > -0.5, (observed - (1.0 - transmit)) * inverse_error, 0.0)
    pull = jnp.where(owned > -0.5, -residual * inverse_error * transmit, 0.0)
    returned = lax.all_to_all(pull, both, split_axis=0, concat_axis=1, tiled=True)[0]

    upper = np.triu(np.ones((rows, rows), np.float32))
    eye = np.eye(rows, dtype=np.float32)
    top_row = np.zeros((16, 4 * rows), np.float32)
    top_row[0, : 2 * rows] = 1.0
    smat = jnp.asarray(
        np.concatenate([np.concatenate([upper, upper, -eye, -eye], 1), top_row], 0).astype(bf16)
    )
    local_sens, tails = pl.pallas_call(
        lambda *refs: scatter_kernel(n_own, *refs),
        grid=(cols // tile,),
        in_specs=[smem] + [full((n_own, LANES))] * 4 + [full(smat.shape)],
        out_specs=[cut(rows), cut(1)],
        out_shape=[grid_shape, line],
        scratch_shapes=[
            pltpu.VMEM((groups * rows, LANES), f32),
            pltpu.VMEM((groups * rows, LANES), f32),
            pltpu.VMEM((2 * LANES, LANES), f32),
        ],
        compiler_params=limit,
        name="scatter",
    )(row, row.astype(f32), lo, share, returned, smat)

    tail_offset = exchange(tails, size, True)
    extinction = prefix + offset.reshape(1, -1)
    sensitivity = density * (local_sens + tail_offset.reshape(1, -1))
    return extinction, sensitivity, residual


def solution(mesh):
    stars = P(("shell", "sky"), None, None)
    owners = P(None, ("shell", "sky"), None)
    return jax.shard_map(
        body,
        mesh=mesh,
        in_specs=(P("shell", "sky"), stars, stars, stars, P(("shell", "sky"), None), owners, owners),
        out_specs=(P("shell", "sky"), P("shell", "sky"), owners),
        check_vma=False,
    )
```

time: 328 us -> 159 us (0.48)
  local copies, waits for them, and re-layouts: 137 us -> 8.72 us
  other arithmetic: 74 us -> 12 us
  Pallas kernels: 0 us -> 48.5 us
  starting transfers between devices: 44.3 us -> 13.8 us
  blocking collectives: 24.1 us -> 41.6 us
  matrix products: 7.15 us -> 0.53 us
  waiting for transfers between devices: 36.5 us -> 31.7 us
    gather x2 -> x0, local copies, waits for them, and re-layouts: 104 us -> none  [the longest x1 52.1 us: body(): dens_at = jnp.take(density.reshape(-1), flat_cell).reshape(slot_shape)]
    pallas_call x0 -> x3, Pallas kernels: none -> 48.5 us  [the longest x1 23.1 us: body(): pl.pallas_call(lambda *refs: density_kernel(n_own, thickness, *refs), gri...]
    scatter-add x1 -> x0, other arithmetic: 47 us -> none  [body(): accumulated = jnp.zeros((2 * cell_count,), jnp.float32).at[both_index].ad...]
    slice x9 -> x1, local copies, waits for them, and re-layouts: 19.7 us -> 1.75 us  [body(): after = lax.ppermute(excitation[:PASSES], 'shell', down)]
    all_to_all x2 -> x4, blocking collectives: 24.1 us -> 41.6 us  [the longest x2 23.9 us: exchange(): lax.all_to_all(spread, 'shell', split_axis=0, concat_axis=0, tiled=True)]
    ppermute x8 -> x2, starting transfers between devices: 22.8 us -> 6.8 us  [the longest x1 5.5 us: body(): before = lax.ppermute(excitation[-PASSES:], 'shell', up)]
    all_to_all x5 -> x2, starting transfers between devices: 21.4 us -> 7.02 us  [exchange(): lax.all_to_all(summed, 'shell', split_axis=0, concat_axis=0, tiled=True)]
    add x5 -> x1, other arithmetic: 13.3 us -> 4.55 us  [body(): extinction = prefix + offset.reshape(1, -1)]
  transfers between devices with their start and end apart: 13 -> 4, of which waited for: 10 -> 4; matrix products, arithmetic and copies ran while one was open for 39% -> 4% of each run, Pallas kernels for 0% -> 0%
where the time goes in v1:
time: 159 us; the launch traced here: 158 us
  Pallas kernels  48.5 us (31%)
  blocking collectives  41.6 us (26%)
  waiting for transfers between devices  31.7 us (20%)
  starting transfers between devices  13.8 us (9%)
  other arithmetic  12 us (8%)
  local copies, waits for them, and re-layouts  8.72 us (5%)
    all_to_all x2, blocking collectives, exchange(): lax.all_to_all(spread, 'shell', split_axis=0, concat_axis=0, tiled=True)  23.9 us
    pallas_call x1, Pallas kernels, body(): pl.pallas_call(lambda *refs: density_kernel(n_own, thickness, *refs), gri...  23.1 us
    pallas_call x1, Pallas kernels, body(): pl.pallas_call(lambda *refs: scatter_kernel(n_own, *refs), grid=(cols //...  19.4 us
    ppermute x1, waiting for transfers between devices, body(): before = lax.ppermute(excitation[-PASSES:], 'shell', up)  11.5 us
    all_to_all x2, waiting for transfers between devices, exchange(): lax.all_to_all(summed, 'shell', split_axis=0, concat_axis=0, tiled=True)  10.9 us
    ppermute x1, waiting for transfers between devices, body(): after = lax.ppermute(excitation[:PASSES], 'shell', down)  9.28 us
    all_to_all x1, blocking collectives, body(): lax.all_to_all(column[None], both, split_axis=1, concat_axis=0, tiled=True)  8.84 us
    all_to_all x1, blocking collectives, body(): lax.all_to_all(pull, both, split_axis=0, concat_axis=1, tiled=True)[0]  8.84 us
  transfers between devices with their start and end apart: 4, of which 4 were waited for; matrix products, arithmetic and copies ran while one was open for 4% of the time, Pallas kernels for 0%

profile of v1, /device:TPU:0, one launch (start us, length us, event | category | flops | bytes accessed | tf_op | source)
XLA Modules:
  0.0 157.7 jit_solution(14501019115379749512)
XLA Ops:
  0.7 1.8 %fusion.13 = (f32[4,32768]{1,0:T(4,128)S(1)}, f32[4,32768]{1,0:T(4,128)S(1)}) fusion(f32[32,32768]{1,0:T(8,128)} %refs_4_.1), kind=kLoop, calls=%fused_computation.32 | loop fusion | bytes 2097152 | tf_op jit(solution)/shard_map/slice | solution.py:212
  2.5 1.3 collective-permute-start.1
  3.8 5.5 %collective-permute-start = (f32[4,32768]{1,0:T(4,128)S(1)}, f32[4,32768]{1,0:T(4,128)S(1)}, u32[]{:S(2)}, u32[]{:S(2)}) collective-permute-start(f32[4,32768]{1,0:T(4,128)S(1)} %get-tuple-element.28), channel_id=1, source_target_pairs={{0,2},{2,4},{4,6},{6,8},{8,10},{10,12},{12,14},{14,16},{16,18},{18... | collective-permute-start | bytes 1572872 | tf_op jit(solution)/shard_map/ppermute | solution.py:211
  9.3 0.7 dynamic-slice_bitcast_fusion.refs_2_
  10.0 0.8 fusion.12
  10.8 9.3 %collective-permute-done.1.refs_6_ = f32[4,32768]{1,0:T(4,128)S(1)} collective-permute-done((f32[4,32768]{1,0:T(4,128)S(1)}, f32[4,32768]{1,0:T(4,128)S(1)}, u32[]{:S(2)}, u32[]{:S(2)}) %collective-permute-start.1) | collective-permute-done | bytes 524320 | tf_op jit(solution)/shard_map/ppermute | solution.py:212
  20.1 11.5 %collective-permute-done.refs_5_ = f32[4,32768]{1,0:T(4,128)S(1)} collective-permute-done((f32[4,32768]{1,0:T(4,128)S(1)}, f32[4,32768]{1,0:T(4,128)S(1)}, u32[]{:S(2)}, u32[]{:S(2)}) %collective-permute-start) | collective-permute-done | bytes 524320 | tf_op jit(solution)/shard_map/ppermute | solution.py:211
  32.3 23.1 %density.1 = (f32[32,32768]{1,0:T(8,128)S(1)}, f32[32,32768]{1,0:T(8,128)}, f32[1,32768]{1,0:T(1,128)S(1)}, f32[32,128]{1,0:T(8,128)S(1)}, f32[32,128]{1,0:T(8,128)S(1)}) custom-call(s32[32,128]{1,0:T(8,128)S(1)} %get-tuple-element.26.refs_0_, s32[32,128]{1,0:T(8,128)S(1)} %get-tuple-element.30.refs_1_.refs_2_, ...), custom_call_target="tpu_custom_call" | custom-call | tf_op jit(solution)/shard_map/density/pallas_call | solution.py:237
  55.3 1.9 %copy-done = f32[32,32768]{1,0:T(8,128)} copy-done((f32[32,32768]{1,0:T(8,128)}, f32[32,32768]{1,0:T(8,128)S(1)}, u32[]{:S(2)}) %copy-start) | copy-done | bytes 4194328
  57.3 13.5 %all_to_all.60 = f32[16,1,2048]{2,1,0:T(1,128)S(1)} all-to-all(f32[16,1,2048]{2,1,0:T(1,128)S(1)} %bitcast.88), channel_id=1, replica_groups=mesh['shell'=16,'sky'=2] {'shell'}, dimensions={0} | all-to-all | bytes 262144 | tf_op jit(solution)/shard_map/all_to_all | solution.py:191
  71.1 0.8 copy.20
  71.9 3.5 %all-to-all-start.1 = ((f32[16,1,2048]{2,1,0:T(1,128)}), f32[16,1,2048]{2,1,0:T(1,128)S(1)}, u32[]{:S(2)}, u32[]{:S(2)}) async-start(f32[16,1,2048]{2,1,0:T(1,128)} %copy.20), calls=%async_computation.1 | async-start | bytes 262144 | tf_op jit(solution)/shard_map/all_to_all | solution.py:196
  75.5 7.7 %all-to-all-done.1 = f32[16,1,2048]{2,1,0:T(1,128)S(1)} async-done(((f32[16,1,2048]{2,1,0:T(1,128)}), f32[16,1,2048]{2,1,0:T(1,128)S(1)}, u32[]{:S(2)}, u32[]{:S(2)}) %all-to-all-start.1) | async-done | bytes 131104 | tf_op jit(solution)/shard_map/all_to_all | solution.py:196
  83.2 6.0 %column.1 = f32[32,128]{1,0:T(8,128)S(1)} custom-call(s32[32,128]{1,0:T(8,128)S(1)} %get-tuple-element.29.refs_0_, s32[32,128]{1,0:T(8,128)S(1)} %get-tuple-element.30.refs_1_.refs_2_, f32[32,128]{1,0:T(8,128)S(1)} %subtract_bitcast_fusion.refs_2_.refs_3_, s32[32,128]{1,0:T(8,128)S(1)} %fusion.9.refs_3_, f32[32,128]{1,0:T(8,128)S(1)} %get-tuple-element.13.refs_4_, ...), custom_call_target="tpu_custom_call" | custom-call | tf_op jit(solution)/shard_map/column/pallas_call | solution.py:254
  89.2 8.8 %all_to_all.61 = f32[1,32,128]{2,0,1:T(1,128)S(1)} all-to-all(f32[1,32,128]{2,0,1:T(1,128)S(1)} %bitcast.91), channel_id=1, replica_groups=mesh['shell'=16,'sky'=2] {'shell','sky'}, dimensions={1} | all-to-all | bytes 32768 | tf_op jit(solution)/shard_map/all_to_all | solution.py:264
  98.7 8.8 %all_to_all.62 = f32[32,1,128]{2,1,0:T(1,128)S(1)} all-to-all(f32[32,1,128]{2,1,0:T(1,128)S(1)} %bitcast.97), channel_id=1, replica_groups=mesh['shell'=16,'sky'=2] {'shell','sky'}, dimensions={0} | all-to-all | bytes 32768 | tf_op jit(solution)/shard_map/all_to_all | solution.py:268
  107.5 19.4 %scatter.1 = (f32[32,32768]{1,0:T(8,128)S(1)}, f32[1,32768]{1,0:T(1,128)S(1)}) custom-call(s32[32,128]{1,0:T(8,128)S(1)} %get-tuple-element.26.refs_0_, f32[32,128]{1,0:T(8,128)S(1)} %get-tuple-element.25.refs_1_, s32[32,128]{1,0:T(8,128)S(1)} %get-tuple-element.30.refs_1_.refs_2_, f32[32,128]{1,0:T(8,128)S(1)} %subtract_bitcast_fusion.refs_2_.refs_3_, ...), custom_call_target="tpu_custom_call" | custom-call | tf_op jit(solution)/shard_map/scatter/pallas_call | solution.py:277
  127.0 2.0 %copy-done.1 = f32[32,32768]{1,0:T(8,128)} copy-done((f32[32,32768]{1,0:T(8,128)}, f32[32,32768]{1,0:T(8,128)S(1)}, u32[]{:S(2)}) %copy-start.1) | copy-done | bytes 4194328
  129.0 10.4 %all_to_all.63 = f32[16,1,2048]{2,1,0:T(1,128)S(1)} all-to-all(f32[16,1,2048]{2,1,0:T(1,128)S(1)} %bitcast.89), channel_id=1, replica_groups=mesh['shell'=16,'sky'=2] {'shell'}, dimensions={0} | all-to-all | bytes 262144 | tf_op jit(solution)/shard_map/all_to_all | solution.py:191
  139.6 0.8 copy.28
  140.4 3.5 %all-to-all-start.5 = ((f32[16,1,2048]{2,1,0:T(1,128)}), f32[16,1,2048]{2,1,0:T(1,128)S(1)}, u32[]{:S(2)}, u32[]{:S(2)}) async-start(f32[16,1,2048]{2,1,0:T(1,128)} %copy.28), calls=%async_computation.5 | async-start | bytes 262144 | tf_op jit(solution)/shard_map/all_to_all | solution.py:196
  143.9 4.5 %broadcast_add_fusion = f32[32,32768]{1,0:T(8,128)} fusion(f32[32,32768]{1,0:T(8,128)} %get-tuple-element.10, f32[32768]{0:T(1024)S(1)} %bitcast.87), kind=kLoop, calls=%fused_computation.3 | loop fusion | flops 1048576 | bytes 8519680 | tf_op jit(solution)/shard_map/add | solution.py:293
  148.5 3.2 %all-to-all-done.5 = f32[16,1,2048]{2,1,0:T(1,128)S(1)} async-done(((f32[16,1,2048]{2,1,0:T(1,128)}), f32[16,1,2048]{2,1,0:T(1,128)S(1)}, u32[]{:S(2)}, u32[]{:S(2)}) %all-to-all-start.5) | async-done | bytes 131104 | tf_op jit(solution)/shard_map/all_to_all | solution.py:196
  151.7 6.0 %add_multiply_fusion = f32[32,32768]{1,0:T(8,128)} fusion(f32[32,32768]{1,0:T(8,128)} %copy-done, f32[32,32768]{1,0:T(8,128)} %copy-done.1, f32[32768]{0:T(1024)S(1)} %bitcast.92), kind=kLoop, calls=%fused_computation | loop fusion | flops 2097152 | bytes 12713984 | tf_op jit(solution)/shard_map/mul | solution.py:294
  (25 shorter events, 2.0 us)
Async XLA Ops:
  0.6 70.2 %copy-start.8 = (f32[16,16]{1,0:T(8,128)S(1)}, f32[16,16]{1,0:T(8,128)}, u32[]{:S(2)}) copy-start(f32[16,16]{1,0:T(8,128)} %constant.66.clone) | copy-start | bytes 3076
  0.6 106.9 %copy-start.2 = (bf16[48,128]{1,0:T(8,128)(2,1)S(1)}, bf16[48,128]{1,0:T(8,128)(2,1)}, u32[]{:S(2)}) copy-start(bf16[48,128]{1,0:T(8,128)(2,1)} %constant.67.clone.refs_5_) | copy-start | bytes 36868
  0.7 74.7 %copy-start.9 = (s32[1,32]{1,0:T(1,128)S(1)}, s32[1,32]{1,0:T(1,128)}, u32[]{:S(2)}) copy-start(s32[1,32]{1,0:T(1,128)} %param.16) | copy-start | bytes 388
  0.7 74.8 %copy-start.6 = (f32[1,32,128]{2,1,0:T(8,128)S(1)}, f32[1,32,128]{2,1,0:T(8,128)}, u32[]{:S(2)}) copy-start(f32[1,32,128]{2,1,0:T(8,128)} %param.15) | copy-start | bytes 49156
  0.7 97.4 %copy-start.4 = (f32[32,1,128]{2,1,0:T(1,128)S(1)}, f32[32,1,128]{2,1,0:T(1,128)}, u32[]{:S(2)}) copy-start(f32[32,1,128]{2,1,0:T(1,128)} %param.18) | copy-start | bytes 49156
  0.7 97.4 %copy-start.5 = (f32[32,1,128]{2,1,0:T(1,128)S(1)}, f32[32,1,128]{2,1,0:T(1,128)}, u32[]{:S(2)}) copy-start(f32[32,1,128]{2,1,0:T(1,128)} %param.17) | copy-start | bytes 49156
  2.5 136.9 %copy-start.7 = (f32[16,16]{1,0:T(8,128)S(1)}, f32[16,16]{1,0:T(8,128)}, u32[]{:S(2)}) copy-start(f32[16,16]{1,0:T(8,128)} %constant.68.clone) | copy-start | bytes 3076
  2.5 17.6 %collective-permute-start.1 = (f32[4,32768]{1,0:T(4,128)S(1)}, f32[4,32768]{1,0:T(4,128)S(1)}, u32[]{:S(2)}, u32[]{:S(2)}) collective-permute-start(f32[4,32768]{1,0:T(4,128)S(1)} %get-tuple-element.27), channel_id=1, source_target_pairs={{2,0},{4,2},{6,4},{8,6},{10,8},{12,10},{14,12},{16,14},{18,16},{20... | collective-permute-start | bytes 1572872 | tf_op jit(solution)/shard_map/ppermute | solution.py:212
  3.8 27.8 %collective-permute-start = (f32[4,32768]{1,0:T(4,128)S(1)}, f32[4,32768]{1,0:T(4,128)S(1)}, u32[]{:S(2)}, u32[]{:S(2)}) collective-permute-start(f32[4,32768]{1,0:T(4,128)S(1)} %get-tuple-element.28), channel_id=1, source_target_pairs={{0,2},{2,4},{4,6},{6,8},{8,10},{10,12},{12,14},{14,16},{16,18},{18... | collective-permute-start | bytes 1572872 | tf_op jit(solution)/shard_map/ppermute | solution.py:211
  31.6 0.7 copy-start.3
  55.3 1.9 %copy-start = (f32[32,32768]{1,0:T(8,128)}, f32[32,32768]{1,0:T(8,128)S(1)}, u32[]{:S(2)}) copy-start(f32[32,32768]{1,0:T(8,128)S(1)} %get-tuple-element.12) | copy-start | bytes 12582916
  71.9 11.3 %all-to-all-start.1 = ((f32[16,1,2048]{2,1,0:T(1,128)}), f32[16,1,2048]{2,1,0:T(1,128)S(1)}, u32[]{:S(2)}, u32[]{:S(2)}) async-start(f32[16,1,2048]{2,1,0:T(1,128)} %copy.20), calls=%async_computation.1 | async-start | bytes 262144 | tf_op jit(solution)/shard_map/all_to_all | solution.py:196
  127.0 2.0 %copy-start.1 = (f32[32,32768]{1,0:T(8,128)}, f32[32,32768]{1,0:T(8,128)S(1)}, u32[]{:S(2)}) copy-start(f32[32,32768]{1,0:T(8,128)S(1)} %get-tuple-element.15) | copy-start | bytes 12582916
  140.4 11.3 %all-to-all-start.5 = ((f32[16,1,2048]{2,1,0:T(1,128)}), f32[16,1,2048]{2,1,0:T(1,128)S(1)}, u32[]{:S(2)}, u32[]{:S(2)}) async-start(f32[16,1,2048]{2,1,0:T(1,128)} %copy.28), calls=%async_computation.5 | async-start | bytes 262144 | tf_op jit(solution)/shard_map/all_to_all | solution.py:196

commit v2 on v1

--- a/solution.py
+++ b/solution.py
@@ -92,32 +92,116 @@
         lax.fori_loop(0, n_own // 2, chunk, 0)
 
 
-def column_kernel(n_own, thickness, hi_ref, lo_ref, share_ref, live_ref, base_ref, slope_ref, off_ref, col_ref):
-    groups = off_ref.shape[0]
-    o1, o2 = split2(off_ref[...])
+def others(count, me, act):
+    def step(k, carry):
+        act(lax.rem(me + k, count))
+        return carry
+
+    lax.fori_loop(1, count, step, 0)
+
+
+def shell_exchange(n, me, upper, src, got, summed, out, sems):
+    send1, recv1, send2, recv2 = sems
+
+    def move(frm, to, send, recv, peer):
+        return pltpu.make_async_remote_copy(
+            src_ref=frm.at[peer], dst_ref=to.at[me], send_sem=send.at[peer], recv_sem=recv.at[me],
+            device_id={"shell": peer}, device_id_type=pl.DeviceIdType.MESH,
+        )
+
+    def landed(frm, to, send, recv, peer):
+        return pltpu.make_async_remote_copy(
+            src_ref=frm.at[peer], dst_ref=to.at[peer], send_sem=send.at[peer], recv_sem=recv.at[peer],
+            device_id={"shell": peer}, device_id_type=pl.DeviceIdType.MESH,
+        )
+
+    others(n, me, lambda p: move(src, got, send1, recv1, p).start())
+    got[pl.ds(me, 1)] = src[pl.ds(me, 1)]
+    others(n, me, lambda p: landed(src, got, send1, recv1, p).wait_recv())
+    total = jnp.zeros(got.shape[1:], jnp.float32)
+    for i in range(n):
+        i = n - 1 - i if upper else i
+        summed[i] = total
+        total = total + got[i]
+    others(n, me, lambda p: move(summed, out, send2, recv2, p).start())
+    out[pl.ds(me, 1)] = summed[pl.ds(me, 1)]
+    others(n, me, lambda p: landed(summed, out, send2, recv2, p).wait_recv())
+    others(n, me, lambda p: move(src, got, send1, recv1, p).wait_send())
+    others(n, me, lambda p: move(summed, out, send2, recv2, p).wait_send())
+
+
+def tail_kernel(n, src, out, got, summed, *sems):
+    me = lax.axis_index("shell")
+    barrier = pltpu.get_barrier_semaphore()
+    others(n, me, lambda p: pl.semaphore_signal(
+        barrier, inc=1, device_id={"shell": p}, device_id_type=pl.DeviceIdType.MESH))
+    pl.semaphore_wait(barrier, n - 1)
+    shell_exchange(n, me, True, src, got, summed, out, sems)
+
+
+def middle_kernel(
+    n, n_sky, thickness, src, hi_ref, lo_ref, share_ref, live_ref, base_ref, slope_ref, obs_ref, inv_ref,
+    off_out, res_ref, back_ref, got, summed, col, owned, pull, *sems,
+):
+    shell = lax.axis_index("shell")
+    me = shell * n_sky + lax.axis_index("sky")
+    n_all = n * n_sky
+    where = lambda p: {"shell": p // n_sky, "sky": lax.rem(p, n_sky)}
+    barrier = pltpu.get_barrier_semaphore()
+    others(n_all, me, lambda p: pl.semaphore_signal(
+        barrier, inc=1, device_id=where(p), device_id_type=pl.DeviceIdType.MESH))
+    pl.semaphore_wait(barrier, n_all - 1)
+    shell_exchange(n, shell, False, src, got, summed, off_out, sems[:4])
+
+    groups = n * src.shape[1]
+    o1, o2 = split2(off_out[...].reshape(groups, LANES))
     table = jnp.concatenate([o1.T, o2.T], 0).astype(jnp.bfloat16)
     tall = lax.broadcasted_iota(jnp.int32, (groups, LANES), 0)
     sub = lax.broadcasted_iota(jnp.int32, (LANES, LANES), 0)
 
-    def chunk(o, carry):
-        hot = (tall == hi_ref[pl.ds(o, 1), :]).astype(jnp.bfloat16)
-        got = jnp.dot(table, hot, preferred_element_type=jnp.float32)
-        got = got[:LANES] + got[LANES:]
-        off = jnp.sum(jnp.where(sub == lo_ref[pl.ds(o, 1), :], got, 0.0), 0, keepdims=True)
-        at = pl.ds(o, 1)
-        col = base_ref[at, :] + off - share_ref[at, :] * thickness * slope_ref[at, :]
-        col_ref[at, :] = jnp.where(live_ref[at, :] > 0, col, -1.0)
+    def chunk(quad, carry):
+        for k in range(4):
+            o = quad * 4 + k
+            at = pl.ds(o, 1)
+            hot = (tall == hi_ref[at, :]).astype(jnp.bfloat16)
+            off = jnp.dot(table, hot, preferred_element_type=jnp.float32)
+            off = off[:LANES] + off[LANES:]
+            off = jnp.sum(jnp.where(sub == lo_ref[at, :], off, 0.0), 0, keepdims=True)
+            value = base_ref[at, :] + off - share_ref[at, :] * thickness * slope_ref[at, :]
+            col[o] = jnp.where(live_ref[at, :] > 0, value, -1.0)
         return carry
 
-    lax.fori_loop(0, n_own, chunk, 0)
+    lax.fori_loop(0, n_all // 4, chunk, 0)
+
+    def move(frm, to, send, recv, peer, slot):
+        return pltpu.make_async_remote_copy(
+            src_ref=frm.at[peer], dst_ref=to.at[slot], send_sem=send.at[peer], recv_sem=recv.at[slot],
+            device_id=where(peer), device_id_type=pl.DeviceIdType.MESH,
+        )
+
+    send3, recv3, send4, recv4 = sems[4:]
+    others(n_all, me, lambda p: move(col, owned, send3, recv3, p, me).start())
+    owned[pl.ds(me, 1)] = col[pl.ds(me, 1)]
+    others(n_all, me, lambda p: move(col, owned, send3, recv3, p, p).wait_recv())
+    column = owned[...]
+    transmit = jnp.exp(-column)
+    inverse = inv_ref[...]
+    residual = jnp.where(column > -0.5, (obs_ref[...] - (1.0 - transmit)) * inverse, 0.0)
+    res_ref[...] = residual
+    pull[...] = jnp.where(column > -0.5, -residual * inverse * transmit, 0.0)
+    others(n_all, me, lambda p: move(pull, back_ref, send4, recv4, p, me).start())
+    back_ref[pl.ds(me, 1)] = pull[pl.ds(me, 1)]
+    others(n_all, me, lambda p: move(pull, back_ref, send4, recv4, p, p).wait_recv())
+    others(n_all, me, lambda p: move(col, owned, send3, recv3, p, me).wait_send())
+    others(n_all, me, lambda p: move(pull, back_ref, send4, recv4, p, me).wait_send())
 
 
 GROUP = 8
 
 
 def scatter_kernel(
-    n_own, row_ref, rows_ref, lo_ref, share_ref, pull_ref, mat_ref,
-    s_ref, tail_ref, imp_tab, near_tab, upd,
+    n_own, row_ref, rows_ref, lo_ref, share_ref, pull_ref, mat_ref, pre_ref, off_ref,
+    s_ref, tail_ref, ext_ref, imp_tab, near_tab, upd,
 ):
     step = pl.program_id(0)
     rows, width = s_ref.shape
@@ -142,7 +226,7 @@
             at = pl.ds(o, 1)
             same = jnp.broadcast_to(rows_ref[at, :], (LANES, LANES))
             same = jnp.logical_and(same == same.T, grouped)
-            pull = pull_ref[at, :]
+            pull = pull_ref[o]
             a1, a2 = split2(jnp.where(same, pull, 0.0))
             b1, b2 = split2(jnp.where(same, pull * share_ref[at, :], 0.0))
             hot = (sub == lo_ref[at, :]).astype(jnp.bfloat16)
@@ -182,18 +266,7 @@
     )
     s_ref[...] = out[:rows]
     tail_ref[...] = out[rows : rows + 1]
-
-
-def exchange(blocks, size, upper):
-    ids = np.arange(size)
-    strict = (ids[:, None] < ids[None, :]) if upper else (ids[:, None] > ids[None, :])
-    spread = blocks.reshape(size, -1)
-    got = lax.all_to_all(spread, "shell", split_axis=0, concat_axis=0, tiled=True)
-    summed = jnp.dot(
-        jnp.asarray(strict, jnp.float32), got,
-        precision=lax.Precision.HIGHEST, preferred_element_type=jnp.float32,
-    )
-    return lax.all_to_all(summed, "shell", split_axis=0, concat_axis=0, tiled=True)
+    ext_ref[...] = pre_ref[...] + off_ref[...]
 
 
 def body(excitation, star_shell, star_pixel, star_fraction, star_count, observed, inverse_error):
@@ -249,23 +322,29 @@
         name="density",
     )(row, lo, mat, tri2, excitation, before, after)
 
-    offset = exchange(sums, size, False)
-
-    column = pl.pallas_call(
-        lambda *refs: column_kernel(n_own, thickness, *refs),
-        in_specs=[vmem] * 7,
-        out_specs=vmem,
-        out_shape=stars,
-        compiler_params=limit,
-        name="column",
-    )(hi, lo, share, live, base, slope, offset.reshape(groups, LANES))
-
-    both = ("shell", "sky")
-    owned = lax.all_to_all(column[None], both, split_axis=1, concat_axis=0, tiled=True)
-    transmit = jnp.exp(-owned)
-    residual = jnp.where(owned > -0.5, (observed - (1.0 - transmit)) * inverse_error, 0.0)
-    pull = jnp.where(owned > -0.5, -residual * inverse_error * transmit, 0.0)
-    returned = lax.all_to_all(pull, both, split_axis=0, concat_axis=1, tiled=True)[0]
+    n_sky = lax.axis_size("sky")
+    n_all = size * n_sky
+    spread = (size, groups // size, LANES)
+    blocks = jax.ShapeDtypeStruct(spread, f32)
+    slots = jax.ShapeDtypeStruct((n_all, 1, LANES), f32)
+    hold = lambda like: pltpu.VMEM(like.shape, f32)
+    dma = lambda k: pltpu.SemaphoreType.DMA((k,))
+
+    def remote(number):
+        return pltpu.CompilerParams(
+            collective_id=number, has_side_effects=True, vmem_limit_bytes=48 * 2**20
+        )
+
+    offset, residual, returned = pl.pallas_call(
+        lambda *refs: middle_kernel(size, n_sky, thickness, *refs),
+        in_specs=[vmem] * 9,
+        out_specs=[vmem] * 3,
+        out_shape=[blocks, slots, slots],
+        scratch_shapes=[hold(blocks), hold(blocks), hold(slots), hold(slots), hold(slots)]
+        + [dma(size)] * 4 + [dma(n_all)] * 4,
+        compiler_params=remote(0),
+        name="middle",
+    )(sums.reshape(spread), hi, lo, share, live, base, slope, observed, inverse_error)
 
     upper = np.triu(np.ones((rows, rows), np.float32))
     eye = np.eye(rows, dtype=np.float32)
@@ -274,12 +353,13 @@
     smat = jnp.asarray(
         np.concatenate([np.concatenate([upper, upper, -eye, -eye], 1), top_row], 0).astype(bf16)
     )
-    local_sens, tails = pl.pallas_call(
+    local_sens, tails, extinction = pl.pallas_call(
         lambda *refs: scatter_kernel(n_own, *refs),
         grid=(cols // tile,),
-        in_specs=[smem] + [full((n_own, LANES))] * 4 + [full(smat.shape)],
-        out_specs=[cut(rows), cut(1)],
-        out_shape=[grid_shape, line],
+        in_specs=[smem] + [full((n_own, LANES))] * 3
+        + [pl.BlockSpec((n_own, 1, LANES), lambda i: (0, 0, 0)), full(smat.shape), cut(rows), cut(1)],
+        out_specs=[cut(rows), cut(1), cut(rows)],
+        out_shape=[grid_shape, line, grid_shape],
         scratch_shapes=[
             pltpu.VMEM((groups * rows, LANES), f32),
             pltpu.VMEM((groups * rows, LANES), f32),
@@ -287,10 +367,17 @@
         ],
         compiler_params=limit,
         name="scatter",
-    )(row, row.astype(f32), lo, share, returned, smat)
-
-    tail_offset = exchange(tails, size, True)
-    extinction = prefix + offset.reshape(1, -1)
+    )(row, row.astype(f32), lo, share, returned, smat, prefix, offset.reshape(1, -1))
+
+    tail_offset = pl.pallas_call(
+        lambda *refs: tail_kernel(size, *refs),
+        in_specs=[vmem],
+        out_specs=vmem,
+        out_shape=blocks,
+        scratch_shapes=[hold(blocks), hold(blocks)] + [dma(size)] * 4,
+        compiler_params=remote(1),
+        name="tails",
+    )(tails.reshape(spread))
     sensitivity = density * (local_sens + tail_offset.reshape(1, -1))
     return extinction, sensitivity, residual
 

time: 159 us -> 129 us (0.81)
  Pallas kernels: 48.5 us -> 92.9 us
  blocking collectives: 41.6 us -> 0 us
  waiting for transfers between devices: 31.7 us -> 19.4 us
  other arithmetic: 12 us -> 4.74 us
  starting transfers between devices: 13.8 us -> 6.8 us
  local copies, waits for them, and re-layouts: 8.72 us -> 3.78 us
    all_to_all x4 -> x0, blocking collectives: 41.6 us -> none  [the longest x2 23.9 us: exchange(): lax.all_to_all(spread, 'shell', split_axis=0, concat_axis=0, tiled=True)]
    pallas_call x1 -> x2, Pallas kernels: 6.04 us -> 43.5 us  [the longest x1 30 us: body(): pl.pallas_call(lambda *refs: middle_kernel(size, n_sky, thickness, *refs)...]
    all_to_all x2 -> x0, waiting for transfers between devices: 10.9 us -> none  [exchange(): lax.all_to_all(summed, 'shell', split_axis=0, concat_axis=0, tiled=True)]
    all_to_all x2 -> x0, starting transfers between devices: 7.02 us -> none  [exchange(): lax.all_to_all(summed, 'shell', split_axis=0, concat_axis=0, tiled=True)]
    pallas_call x1, Pallas kernels: 19.4 us -> 26.3 us  [body(): pl.pallas_call(lambda *refs: scatter_kernel(n_own, *refs), grid=(cols //...]
    add x1 -> x0, other arithmetic: 4.55 us -> none  [body(): extinction = prefix + offset.reshape(1, -1)]
    mul x1, other arithmetic: 5.98 us -> 2.54 us  [body(): sensitivity = density * (local_sens + tail_offset.reshape(1, -1))]
    unnamed x20 -> x9, local copies, waits for them, and re-layouts: 4.65 us -> 1.32 us
  transfers between devices with their start and end apart: 4 -> 2, of which waited for: 4 -> 2; matrix products, arithmetic and copies ran while one was open for 4% -> 2% of each run, Pallas kernels for 0% -> 0%
where the time goes in v2:
time: 129 us; the launch traced here: 128 us
  Pallas kernels  92.9 us (72%)
  waiting for transfers between devices  19.4 us (15%)
  starting transfers between devices  6.8 us (5%)
  other arithmetic  4.74 us (4%)
  local copies, waits for them, and re-layouts  3.78 us (3%)
    pallas_call x1, Pallas kernels, body(): pl.pallas_call(lambda *refs: middle_kernel(size, n_sky, thickness, *refs)...  30 us
    pallas_call x1, Pallas kernels, body(): pl.pallas_call(lambda *refs: scatter_kernel(n_own, *refs), grid=(cols //...  26.3 us
    pallas_call x1, Pallas kernels, body(): pl.pallas_call(lambda *refs: density_kernel(n_own, thickness, *refs), gri...  23.1 us
    pallas_call x1, Pallas kernels, body(): pl.pallas_call(lambda *refs: tail_kernel(size, *refs), in_specs=[vmem], o...  13.6 us
    ppermute x1, waiting for transfers between devices, body(): before = lax.ppermute(excitation[-PASSES:], 'shell', up)  11.5 us
    ppermute x1, waiting for transfers between devices, body(): after = lax.ppermute(excitation[:PASSES], 'shell', down)  7.84 us
    ppermute x1, starting transfers between devices, body(): before = lax.ppermute(excitation[-PASSES:], 'shell', up)  5.5 us
  transfers between devices with their start and end apart: 2, of which 2 were waited for; matrix products, arithmetic and copies ran while one was open for 2% of the time, Pallas kernels for 0%

profile of v2, /device:TPU:0, one launch (start us, length us, event | category | flops | bytes accessed | tf_op | source)
XLA Modules:
  0.0 128.3 jit_solution(14916576994502483651)
XLA Ops:
  0.6 0.0 copy-start.2
  0.6 0.0 copy-start.1
  0.7 0.0 copy-start
  0.7 1.7 %fusion.5 = (f32[4,32768]{1,0:T(4,128)S(1)}, f32[4,32768]{1,0:T(4,128)S(1)}) fusion(f32[32,32768]{1,0:T(8,128)} %refs_4_.1), kind=kLoop, calls=%fused_computation.17 | loop fusion | bytes 2097152 | tf_op jit(solution)/shard_map/slice | solution.py:285
  2.4 1.3 %collective-permute-start.1 = (f32[4,32768]{1,0:T(4,128)S(1)}, f32[4,32768]{1,0:T(4,128)S(1)}, u32[]{:S(2)}, u32[]{:S(2)}) collective-permute-start(f32[4,32768]{1,0:T(4,128)S(1)} %get-tuple-element.27), channel_id=1, source_target_pairs={{2,0},{4,2},{6,4},{8,6},{10,8},{12,10},{14,12},{16,14},{18,16},{20... | collective-permute-start | bytes 1572872 | tf_op jit(solution)/shard_map/ppermute | solution.py:285
  3.7 5.5 %collective-permute-start = (f32[4,32768]{1,0:T(4,128)S(1)}, f32[4,32768]{1,0:T(4,128)S(1)}, u32[]{:S(2)}, u32[]{:S(2)}) collective-permute-start(f32[4,32768]{1,0:T(4,128)S(1)} %get-tuple-element.28), channel_id=1, source_target_pairs={{0,2},{2,4},{4,6},{6,8},{8,10},{10,12},{12,14},{14,16},{16,18},{18... | collective-permute-start | bytes 1572872 | tf_op jit(solution)/shard_map/ppermute | solution.py:284
  9.2 0.7 fusion.1.refs_4_
  10.0 0.7 dynamic-slice_bitcast_fusion.refs_2_
  10.7 0.7 subtract_bitcast_fusion.refs_3_
  11.4 0.8 fusion.4
  12.2 7.8 %collective-permute-done.1.refs_6_ = f32[4,32768]{1,0:T(4,128)S(1)} collective-permute-done((f32[4,32768]{1,0:T(4,128)S(1)}, f32[4,32768]{1,0:T(4,128)S(1)}, u32[]{:S(2)}, u32[]{:S(2)}) %collective-permute-start.1) | collective-permute-done | bytes 524320 | tf_op jit(solution)/shard_map/ppermute | solution.py:285
  20.0 11.5 %collective-permute-done.refs_5_ = f32[4,32768]{1,0:T(4,128)S(1)} collective-permute-done((f32[4,32768]{1,0:T(4,128)S(1)}, f32[4,32768]{1,0:T(4,128)S(1)}, u32[]{:S(2)}, u32[]{:S(2)}) %collective-permute-start) | collective-permute-done | bytes 524320 | tf_op jit(solution)/shard_map/ppermute | solution.py:284
  31.5 0.0 copy-start.3
  31.5 0.7 copy-done.3
  32.2 23.1 %density.1 = (f32[32,32768]{1,0:T(8,128)S(1)}, f32[32,32768]{1,0:T(8,128)}, f32[1,32768]{1,0:T(1,128)S(1)}, f32[32,128]{1,0:T(8,128)S(1)}, f32[32,128]{1,0:T(8,128)S(1)}) custom-call(s32[32,128]{1,0:T(8,128)S(1)} %get-tuple-element.26.refs_0_, s32[32,128]{1,0:T(8,128)S(1)} %get-tuple-element.30.refs_1_.refs_2_, ...), custom_call_target="tpu_custom_call" | custom-call | tf_op jit(solution)/shard_map/density/pallas_call | solution.py:310
  55.3 0.0 copy-done.1
  55.3 0.0 copy-done
  55.3 30.0 %middle.1 = (f32[16,16,128]{2,1,0:T(8,128)S(1)}, f32[32,1,128]{2,1,0:T(1,128)S(1)}, f32[32,1,128]{2,1,0:T(1,128)S(1)}) custom-call(f32[16,16,128]{2,1,0:T(8,128)S(1)} %bitcast.43, s32[32,128]{1,0:T(8,128)S(1)} %get-tuple-element.29.refs_1_, s32[32,128]{1,0:T(8,128)S(1)} %get-tuple-element.30.refs_1_.refs_2_, f32[32,128]{1,0:T(8,128)S(1)} %subtract_bitcast_fusion.refs_3_, ...), custom_call_target="tpu_custom_call" | custom-call | tf_op jit(solution)/shard_map/middle/pallas_call | solution.py:338
  85.3 0.0 copy-done.2
  85.3 26.3 %scatter.1 = (f32[32,32768]{1,0:T(8,128)S(1)}, f32[1,32768]{1,0:T(1,128)S(1)}, f32[32,32768]{1,0:T(8,128)}) custom-call(s32[32,128]{1,0:T(8,128)S(1)} %get-tuple-element.26.refs_0_, f32[32,128]{1,0:T(8,128)S(1)} %get-tuple-element.25.refs_1_, s32[32,128]{1,0:T(8,128)S(1)} %get-tuple-element.30.refs_1_.refs_2_, f32[32,128]{1,0:T(8,128)S(1)} %subtract_bitcast_fusion.refs_3_, ...), custom_call_target="tpu_custom_call" | custom-call | tf_op jit(solution)/shard_map/scatter/pallas_call | solution.py:356
  111.5 13.6 %tails.1 = f32[16,16,128]{2,1,0:T(8,128)S(1)} custom-call(f32[16,16,128]{2,1,0:T(8,128)S(1)} %bitcast.44), custom_call_target="tpu_custom_call" | custom-call | tf_op jit(solution)/shard_map/tails/pallas_call | solution.py:372
  125.1 2.5 %add_multiply_fusion = f32[32,32768]{1,0:T(8,128)} fusion(f32[32,32768]{1,0:T(8,128)S(1)} %get-tuple-element.21, f32[32,32768]{1,0:T(8,128)S(1)} %get-tuple-element.22, f32[32768]{0:T(1024)S(1)} %bitcast.41), kind=kLoop, calls=%fused_computation | loop fusion | flops 2097152 | bytes 12713984 | tf_op jit(solution)/shard_map/mul | solution.py:381
  127.6 0.6 copy.14
Async XLA Ops:
  0.6 84.6 %copy-start.2 = (bf16[48,128]{1,0:T(8,128)(2,1)S(1)}, bf16[48,128]{1,0:T(8,128)(2,1)}, u32[]{:S(2)}) copy-start(bf16[48,128]{1,0:T(8,128)(2,1)} %constant.57.clone.refs_5_) | copy-start | bytes 36868
  0.6 54.6 %copy-start.1 = (f32[32,1,128]{2,1,0:T(1,128)S(1)}, f32[32,1,128]{2,1,0:T(1,128)}, u32[]{:S(2)}) copy-start(f32[32,1,128]{2,1,0:T(1,128)} %refs_8_.1) | copy-start | bytes 49156
  0.7 54.6 %copy-start = (f32[32,1,128]{2,1,0:T(1,128)S(1)}, f32[32,1,128]{2,1,0:T(1,128)}, u32[]{:S(2)}) copy-start(f32[32,1,128]{2,1,0:T(1,128)} %refs_7_.1) | copy-start | bytes 49156
  2.4 17.6 %collective-permute-start.1 = (f32[4,32768]{1,0:T(4,128)S(1)}, f32[4,32768]{1,0:T(4,128)S(1)}, u32[]{:S(2)}, u32[]{:S(2)}) collective-permute-start(f32[4,32768]{1,0:T(4,128)S(1)} %get-tuple-element.27), channel_id=1, source_target_pairs={{2,0},{4,2},{6,4},{8,6},{10,8},{12,10},{14,12},{16,14},{18,16},{20... | collective-permute-start | bytes 1572872 | tf_op jit(solution)/shard_map/ppermute | solution.py:285
  3.7 27.8 %collective-permute-start = (f32[4,32768]{1,0:T(4,128)S(1)}, f32[4,32768]{1,0:T(4,128)S(1)}, u32[]{:S(2)}, u32[]{:S(2)}) collective-permute-start(f32[4,32768]{1,0:T(4,128)S(1)} %get-tuple-element.28), channel_id=1, source_target_pairs={{0,2},{2,4},{4,6},{6,8},{8,10},{10,12},{12,14},{14,16},{16,18},{18... | collective-permute-start | bytes 1572872 | tf_op jit(solution)/shard_map/ppermute | solution.py:284
  31.5 0.7 copy-start.3

commit v3 on v2

--- a/solution.py
+++ b/solution.py
@@ -36,62 +36,6 @@
     return np.concatenate([local, local, halo, halo], 1).astype(np.float32)
 
 
-def density_kernel(
-    n_own, thickness, row_ref, lo_ref, mat_ref, tri_ref, exc_ref, bef_ref, aft_ref,
-    dens_ref, pre_ref, sum_ref, base_ref, slope_ref, pre_tab, dens_tab, got,
-):
-    step = pl.program_id(0)
-    rows, width = exc_ref.shape
-    blocks = width // LANES
-    e1, e2 = split2(exc_ref[...])
-    h1, h2 = split2(jnp.concatenate([bef_ref[...], aft_ref[...]], 0))
-    stacked = jnp.concatenate([e1, e2, h1, h2], 0).astype(jnp.bfloat16)
-    both = jnp.dot(mat_ref[...], stacked, preferred_element_type=jnp.float32)
-    dens = jnp.exp(both[:rows] + both[rows:])
-    d1, d2 = split2(dens)
-    pre = thickness * jnp.dot(
-        tri_ref[...],
-        jnp.concatenate([d1, d2], 0).astype(jnp.bfloat16),
-        preferred_element_type=jnp.float32,
-    )
-    dens_ref[...] = dens
-    pre_ref[...] = pre
-    sum_ref[...] = pre[rows - 1 : rows]
-    for b in range(blocks):
-        at = pl.ds(pl.multiple_of((step * blocks + b) * rows, rows), rows)
-        pre_tab[at, :] = pre[:, b * LANES : (b + 1) * LANES]
-        dens_tab[at, :] = dens[:, b * LANES : (b + 1) * LANES]
-
-    @pl.when(step == pl.num_programs(0) - 1)
-    def _():
-        lane = lax.broadcasted_iota(jnp.int32, (LANES, LANES), 1)
-        sub = lax.broadcasted_iota(jnp.int32, (LANES, LANES), 0)
-
-        def chunk(pair, carry):
-            for k in range(2):
-                o = pair * 2 + k
-                for c in range(LANES):
-                    at = row_ref[o, c]
-                    got[k, c : c + 1, :] = pre_tab[pl.ds(at, 1), :]
-                    got[k, LANES + c : LANES + c + 1, :] = dens_tab[pl.ds(at, 1), :]
-            for k in range(2):
-                o = pair * 2 + k
-                hot = (sub == lo_ref[pl.ds(o, 1), :]).astype(jnp.bfloat16)
-                g1, g2 = split2(got[k])
-                picked = jnp.dot(
-                    jnp.concatenate([g1, g2], 0).astype(jnp.bfloat16),
-                    hot,
-                    preferred_element_type=jnp.float32,
-                )
-                p = picked[:LANES] + picked[2 * LANES : 3 * LANES]
-                d = picked[LANES : 2 * LANES] + picked[3 * LANES :]
-                base_ref[pl.ds(o, 1), :] = jnp.sum(jnp.where(sub == lane, p, 0.0), 0, keepdims=True)
-                slope_ref[pl.ds(o, 1), :] = jnp.sum(jnp.where(sub == lane, d, 0.0), 0, keepdims=True)
-            return carry
-
-        lax.fori_loop(0, n_own // 2, chunk, 0)
-
-
 def others(count, me, act):
     def step(k, carry):
         act(lax.rem(me + k, count))
@@ -100,34 +44,30 @@
     lax.fori_loop(1, count, step, 0)
 
 
-def shell_exchange(n, me, upper, src, got, summed, out, sems):
+def shell_exchange(n, me, upper, src, got, summed, out, sems, meanwhile=lambda half: None):
     send1, recv1, send2, recv2 = sems
 
-    def move(frm, to, send, recv, peer):
+    def move(frm, to, send, recv, peer, slot):
         return pltpu.make_async_remote_copy(
-            src_ref=frm.at[peer], dst_ref=to.at[me], send_sem=send.at[peer], recv_sem=recv.at[me],
+            src_ref=frm.at[peer], dst_ref=to.at[slot], send_sem=send.at[peer], recv_sem=recv.at[slot],
             device_id={"shell": peer}, device_id_type=pl.DeviceIdType.MESH,
         )
 
-    def landed(frm, to, send, recv, peer):
-        return pltpu.make_async_remote_copy(
-            src_ref=frm.at[peer], dst_ref=to.at[peer], send_sem=send.at[peer], recv_sem=recv.at[peer],
-            device_id={"shell": peer}, device_id_type=pl.DeviceIdType.MESH,
-        )
-
-    others(n, me, lambda p: move(src, got, send1, recv1, p).start())
+    others(n, me, lambda p: move(src, got, send1, recv1, p, me).start())
     got[pl.ds(me, 1)] = src[pl.ds(me, 1)]
-    others(n, me, lambda p: landed(src, got, send1, recv1, p).wait_recv())
+    meanwhile(0)
+    others(n, me, lambda p: move(src, got, send1, recv1, p, p).wait_recv())
     total = jnp.zeros(got.shape[1:], jnp.float32)
     for i in range(n):
         i = n - 1 - i if upper else i
         summed[i] = total
         total = total + got[i]
-    others(n, me, lambda p: move(summed, out, send2, recv2, p).start())
+    others(n, me, lambda p: move(summed, out, send2, recv2, p, me).start())
     out[pl.ds(me, 1)] = summed[pl.ds(me, 1)]
-    others(n, me, lambda p: landed(summed, out, send2, recv2, p).wait_recv())
-    others(n, me, lambda p: move(src, got, send1, recv1, p).wait_send())
-    others(n, me, lambda p: move(summed, out, send2, recv2, p).wait_send())
+    meanwhile(1)
+    others(n, me, lambda p: move(summed, out, send2, recv2, p, p).wait_recv())
+    others(n, me, lambda p: move(src, got, send1, recv1, p, me).wait_send())
+    others(n, me, lambda p: move(summed, out, send2, recv2, p, me).wait_send())
 
 
 def tail_kernel(n, src, out, got, summed, *sems):
@@ -139,25 +79,129 @@
     shell_exchange(n, me, True, src, got, summed, out, sems)
 
 
-def middle_kernel(
-    n, n_sky, thickness, src, hi_ref, lo_ref, share_ref, live_ref, base_ref, slope_ref, obs_ref, inv_ref,
-    off_out, res_ref, back_ref, got, summed, col, owned, pull, *sems,
+def field_kernel(
+    n, n_sky, thickness, row_ref, exc_ref, mat_ref, tri_ref, hi_ref, lo_ref, share_ref, live_ref, obs_ref, inv_ref,
+    dens_out, pre_out, off_out, res_ref, back_ref,
+    last4, first4, before, after, dens_nat, pre_nat, pre_tab, dens_tab, got_rows, base_ref, slope_ref,
+    src, got, summed, col, owned, pull, out_sems, up_send, up_recv, down_send, down_recv, *sems,
 ):
     shell = lax.axis_index("shell")
     me = shell * n_sky + lax.axis_index("sky")
     n_all = n * n_sky
+    rows, cols = exc_ref.shape
+    tiles, _, width = last4.shape
+    blocks = width // LANES
+    part = src.shape[1]
     where = lambda p: {"shell": p // n_sky, "sky": lax.rem(p, n_sky)}
     barrier = pltpu.get_barrier_semaphore()
     others(n_all, me, lambda p: pl.semaphore_signal(
         barrier, inc=1, device_id=where(p), device_id_type=pl.DeviceIdType.MESH))
+    for t in range(tiles):
+        at = slice(t * width, (t + 1) * width)
+        last4[t] = exc_ref[rows - PASSES :, at]
+        first4[t] = exc_ref[:PASSES, at]
+
+    @pl.when(shell == 0)
+    def _():
+        before[...] = jnp.zeros(before.shape, jnp.float32)
+
+    @pl.when(shell == n - 1)
+    def _():
+        after[...] = jnp.zeros(after.shape, jnp.float32)
+
     pl.semaphore_wait(barrier, n_all - 1)
-    shell_exchange(n, shell, False, src, got, summed, off_out, sems[:4])
+
+    def upward(t):
+        return pltpu.make_async_remote_copy(
+            src_ref=last4.at[t], dst_ref=before.at[t], send_sem=up_send.at[t], recv_sem=up_recv.at[t],
+            device_id={"shell": lax.rem(shell + 1, n)}, device_id_type=pl.DeviceIdType.MESH,
+        )
+
+    def downward(t):
+        return pltpu.make_async_remote_copy(
+            src_ref=first4.at[t], dst_ref=after.at[t], send_sem=down_send.at[t], recv_sem=down_recv.at[t],
+            device_id={"shell": lax.rem(shell + n - 1, n)}, device_id_type=pl.DeviceIdType.MESH,
+        )
+
+    has_up, has_down = shell < n - 1, shell > 0
+
+    def send(t, carry):
+        pl.when(has_up)(lambda: upward(t).start())
+        pl.when(has_down)(lambda: downward(t).start())
+        return carry
+
+    lax.fori_loop(0, tiles, send, 0)
+
+    def outward(t):
+        at = pl.ds(pl.multiple_of(t * width, width), width)
+        return (
+            pltpu.make_async_copy(dens_nat.at[t], dens_out.at[:, at], out_sems.at[0, t]),
+            pltpu.make_async_copy(pre_nat.at[t], pre_out.at[:, at], out_sems.at[1, t]),
+        )
+
+    def tile(t, carry):
+        pl.when(has_down)(lambda: upward(t).wait_recv())
+        pl.when(has_up)(lambda: downward(t).wait_recv())
+        e1, e2 = split2(exc_ref[:, pl.ds(pl.multiple_of(t * width, width), width)])
+        h1, h2 = split2(jnp.concatenate([before[t], after[t]], 0))
+        stacked = jnp.concatenate([e1, e2, h1, h2], 0).astype(jnp.bfloat16)
+        both = jnp.dot(mat_ref[...], stacked, preferred_element_type=jnp.float32)
+        dens = jnp.exp(both[:rows] + both[rows:])
+        d1, d2 = split2(dens)
+        pre = thickness * jnp.dot(
+            tri_ref[...],
+            jnp.concatenate([d1, d2], 0).astype(jnp.bfloat16),
+            preferred_element_type=jnp.float32,
+        )
+        dens_nat[t] = dens
+        pre_nat[t] = pre
+        for b in range(blocks):
+            g = t * blocks + b
+            at = pl.ds(pl.multiple_of(g * rows, rows), rows)
+            pre_tab[at, :] = pre[:, b * LANES : (b + 1) * LANES]
+            dens_tab[at, :] = dens[:, b * LANES : (b + 1) * LANES]
+            src[g // part, pl.ds(lax.rem(g, part), 1), :] = pre[rows - 1 :, b * LANES : (b + 1) * LANES]
+        for copy in outward(t):
+            copy.start()
+        return carry
+
+    lax.fori_loop(0, tiles, tile, 0)
+    lane = lax.broadcasted_iota(jnp.int32, (LANES, LANES), 1)
+    sub = lax.broadcasted_iota(jnp.int32, (LANES, LANES), 0)
+
+    def pick(pair, carry):
+        for k in range(2):
+            o = pair * 2 + k
+            for c in range(LANES):
+                at = row_ref[o, c]
+                got_rows[k, c : c + 1, :] = pre_tab[pl.ds(at, 1), :]
+                got_rows[k, LANES + c : LANES + c + 1, :] = dens_tab[pl.ds(at, 1), :]
+        for k in range(2):
+            o = pair * 2 + k
+            hot = (sub == lo_ref[pl.ds(o, 1), :]).astype(jnp.bfloat16)
+            g1, g2 = split2(got_rows[k])
+            picked = jnp.dot(
+                jnp.concatenate([g1, g2], 0).astype(jnp.bfloat16),
+                hot,
+                preferred_element_type=jnp.float32,
+            )
+            p = picked[:LANES] + picked[2 * LANES : 3 * LANES]
+            d = picked[LANES : 2 * LANES] + picked[3 * LANES :]
+            base_ref[pl.ds(o, 1), :] = jnp.sum(jnp.where(sub == lane, p, 0.0), 0, keepdims=True)
+            slope_ref[pl.ds(o, 1), :] = jnp.sum(jnp.where(sub == lane, d, 0.0), 0, keepdims=True)
+        return carry
+
+    pairs = n_all // 2
+    cut = [0, pairs // 2, pairs]
+    shell_exchange(
+        n, shell, False, src, got, summed, off_out, sems[:4],
+        lambda half: lax.fori_loop(cut[half], cut[half + 1], pick, 0),
+    )
 
     groups = n * src.shape[1]
     o1, o2 = split2(off_out[...].reshape(groups, LANES))
     table = jnp.concatenate([o1.T, o2.T], 0).astype(jnp.bfloat16)
     tall = lax.broadcasted_iota(jnp.int32, (groups, LANES), 0)
-    sub = lax.broadcasted_iota(jnp.int32, (LANES, LANES), 0)
 
     def chunk(quad, carry):
         for k in range(4):
@@ -195,8 +239,18 @@
     others(n_all, me, lambda p: move(col, owned, send3, recv3, p, me).wait_send())
     others(n_all, me, lambda p: move(pull, back_ref, send4, recv4, p, me).wait_send())
 
+    def drain(t, carry):
+        for copy in outward(t):
+            copy.wait()
+        pl.when(has_up)(lambda: upward(t).wait_send())
+        pl.when(has_down)(lambda: downward(t).wait_send())
+        return carry
+
+    lax.fori_loop(0, tiles, drain, 0)
+
 
 GROUP = 8
+CHUNKS = 4
 
 
 def scatter_kernel(
@@ -206,6 +260,7 @@
     step = pl.program_id(0)
     rows, width = s_ref.shape
     blocks = width // LANES
+    first_phase = n_own // CHUNKS
 
     @pl.when(step == 0)
     def _():
@@ -218,6 +273,10 @@
             return carry
 
         lax.fori_loop(0, total // 256, clear, 0)
+
+    @pl.when(step < first_phase)
+    def _():
+        ext_ref[...] = pre_ref[...] + off_ref[...]
         sub = lax.broadcasted_iota(jnp.int32, (LANES, LANES), 0)
         lane = lax.broadcasted_iota(jnp.int32, (LANES, LANES), 1)
         grouped = sub // GROUP == lane // GROUP
@@ -248,25 +307,26 @@
                     near_tab[pl.ds(w, 1), :] = b
             return carry
 
-        lax.fori_loop(0, n_own, chunk, 0)
+        lax.fori_loop(step * CHUNKS, (step + 1) * CHUNKS, chunk, 0)
 
     def natural(tab):
         parts = []
         for b in range(blocks):
-            at = pl.ds(pl.multiple_of((step * blocks + b) * rows, rows), rows)
+            at = pl.ds(pl.multiple_of(((step - first_phase) * blocks + b) * rows, rows), rows)
             parts.append(tab[at, :])
         return jnp.concatenate(parts, 1)
 
-    i1, i2 = split2(natural(imp_tab))
-    n1, n2 = split2(natural(near_tab))
-    out = jnp.dot(
-        mat_ref[...],
-        jnp.concatenate([i1, i2, n1, n2], 0).astype(jnp.bfloat16),
-        preferred_element_type=jnp.float32,
-    )
-    s_ref[...] = out[:rows]
-    tail_ref[...] = out[rows : rows + 1]
-    ext_ref[...] = pre_ref[...] + off_ref[...]
+    @pl.when(step >= first_phase)
+    def _():
+        i1, i2 = split2(natural(imp_tab))
+        n1, n2 = split2(natural(near_tab))
+        out = jnp.dot(
+            mat_ref[...],
+            jnp.concatenate([i1, i2, n1, n2], 0).astype(jnp.bfloat16),
+            preferred_element_type=jnp.float32,
+        )
+        s_ref[...] = out[:rows]
+        tail_ref[...] = out[rows : rows + 1]
 
 
 def body(excitation, star_shell, star_pixel, star_fraction, star_count, observed, inverse_error):
@@ -279,11 +339,6 @@
     tile = min(TILE, cols)
     f32, bf16 = jnp.float32, jnp.bfloat16
 
-    up = [(i, i + 1) for i in range(size - 1)]
-    down = [(i + 1, i) for i in range(size - 1)]
-    before = lax.ppermute(excitation[-PASSES:], "shell", up)
-    after = lax.ppermute(excitation[:PASSES], "shell", down)
-
     pixel = star_pixel[0]
     hi, lo = pixel // LANES, pixel % LANES
     row = hi * rows + star_shell[0]
@@ -301,26 +356,10 @@
     smem = pl.BlockSpec(memory_space=pltpu.SMEM)
     vmem = pl.BlockSpec(memory_space=pltpu.VMEM)
     full = lambda shape: pl.BlockSpec(shape, lambda i: (0, 0))
-    cut = lambda r: pl.BlockSpec((r, tile), lambda i: (0, i))
     stars = jax.ShapeDtypeStruct((n_own, LANES), f32)
     grid_shape = jax.ShapeDtypeStruct((rows, cols), f32)
     line = jax.ShapeDtypeStruct((1, cols), f32)
     limit = pltpu.CompilerParams(vmem_limit_bytes=48 * 2**20)
-
-    density, prefix, sums, base, slope = pl.pallas_call(
-        lambda *refs: density_kernel(n_own, thickness, *refs),
-        grid=(cols // tile,),
-        in_specs=[smem, full((n_own, LANES)), full(mat.shape), full(tri2.shape), cut(rows), cut(PASSES), cut(PASSES)],
-        out_specs=[cut(rows), cut(rows), cut(1), full((n_own, LANES)), full((n_own, LANES))],
-        out_shape=[grid_shape, grid_shape, line, stars, stars],
-        scratch_shapes=[
-            pltpu.VMEM((groups * rows, LANES), f32),
-            pltpu.VMEM((groups * rows, LANES), f32),
-            pltpu.VMEM((2, 2 * LANES, LANES), f32),
-        ],
-        compiler_params=limit,
-        name="density",
-    )(row, lo, mat, tri2, excitation, before, after)
 
     n_sky = lax.axis_size("sky")
     n_all = size * n_sky
@@ -335,16 +374,23 @@
             collective_id=number, has_side_effects=True, vmem_limit_bytes=48 * 2**20
         )
 
-    offset, residual, returned = pl.pallas_call(
-        lambda *refs: middle_kernel(size, n_sky, thickness, *refs),
-        in_specs=[vmem] * 9,
-        out_specs=[vmem] * 3,
-        out_shape=[blocks, slots, slots],
-        scratch_shapes=[hold(blocks), hold(blocks), hold(slots), hold(slots), hold(slots)]
-        + [dma(size)] * 4 + [dma(n_all)] * 4,
+    tiles = cols // tile
+    hbm = pl.BlockSpec(memory_space=pl.ANY)
+    edge = pltpu.VMEM((tiles, PASSES, tile), f32)
+    nat = pltpu.VMEM((tiles, rows, tile), f32)
+    tab = pltpu.VMEM((groups * rows, LANES), f32)
+    density, prefix, offset, residual, returned = pl.pallas_call(
+        lambda *refs: field_kernel(size, n_sky, thickness, *refs),
+        in_specs=[smem] + [vmem] * 9,
+        out_specs=[hbm] * 2 + [vmem] * 3,
+        out_shape=[grid_shape, grid_shape, blocks, slots, slots],
+        scratch_shapes=[edge] * 4 + [nat] * 2 + [tab] * 2
+        + [pltpu.VMEM((2, 2 * LANES, LANES), f32), hold(stars), hold(stars)]
+        + [hold(blocks)] * 3 + [hold(slots)] * 3
+        + [pltpu.SemaphoreType.DMA((2, tiles))] + [dma(tiles)] * 4 + [dma(size)] * 4 + [dma(n_all)] * 4,
         compiler_params=remote(0),
-        name="middle",
-    )(sums.reshape(spread), hi, lo, share, live, base, slope, observed, inverse_error)
+        name="field",
+    )(row, excitation, mat, tri2, hi, lo, share, live, observed, inverse_error)
 
     upper = np.triu(np.ones((rows, rows), np.float32))
     eye = np.eye(rows, dtype=np.float32)
@@ -353,12 +399,17 @@
     smat = jnp.asarray(
         np.concatenate([np.concatenate([upper, upper, -eye, -eye], 1), top_row], 0).astype(bf16)
     )
+    early = n_own // CHUNKS
+    ext_tile = cols // early
+    out_tile = min(2 * TILE, cols)
+    first = lambda r: pl.BlockSpec((r, ext_tile), lambda i: (0, jnp.minimum(i, early - 1)))
+    second = lambda r: pl.BlockSpec((r, out_tile), lambda i: (0, jnp.maximum(i - early, 0)))
     local_sens, tails, extinction = pl.pallas_call(
         lambda *refs: scatter_kernel(n_own, *refs),
-        grid=(cols // tile,),
+        grid=(early + cols // out_tile,),
         in_specs=[smem] + [full((n_own, LANES))] * 3
-        + [pl.BlockSpec((n_own, 1, LANES), lambda i: (0, 0, 0)), full(smat.shape), cut(rows), cut(1)],
-        out_specs=[cut(rows), cut(1), cut(rows)],
+        + [pl.BlockSpec((n_own, 1, LANES), lambda i: (0, 0, 0)), full(smat.shape), first(rows), first(1)],
+        out_specs=[second(rows), second(1), first(rows)],
         out_shape=[grid_shape, line, grid_shape],
         scratch_shapes=[
             pltpu.VMEM((groups * rows, LANES), f32),

time: 129 us -> 105 us (0.81)
  waiting for transfers between devices: 19.4 us -> 0 us
  starting transfers between devices: 6.8 us -> 0 us
  Pallas kernels: 92.9 us -> 95.1 us
    ppermute x2 -> x0, waiting for transfers between devices: 19.4 us -> none  [the longest x1 11.5 us: body(): before = lax.ppermute(excitation[-PASSES:], 'shell', up)]
    ppermute x2 -> x0, starting transfers between devices: 6.8 us -> none  [the longest x1 5.5 us: body(): before = lax.ppermute(excitation[-PASSES:], 'shell', up)]
    slice x1 -> x0, local copies, waits for them, and re-layouts: 1.74 us -> none  [body(): after = lax.ppermute(excitation[:PASSES], 'shell', down)]
    pallas_call x3 -> x2, Pallas kernels: 79.3 us -> 81 us  [the longest x1 60.6 us: body(): pl.pallas_call(lambda *refs: field_kernel(size, n_sky, thickness, *refs),...]
    unnamed x9, local copies, waits for them, and re-layouts: 1.32 us -> 2.74 us
  transfers between devices with their start and end apart: 2 -> 0, of which waited for: 2 -> 0; matrix products, arithmetic and copies ran while one was open for 2% -> 0% of each run, Pallas kernels for 0% -> 0%
where the time goes in v3:
time: 105 us; the launch traced here: 104 us
  Pallas kernels  95.1 us (91%)
  other arithmetic  4.74 us (5%)
  local copies, waits for them, and re-layouts  3.46 us (3%)
    pallas_call x1, Pallas kernels, body(): pl.pallas_call(lambda *refs: field_kernel(size, n_sky, thickness, *refs),...  60.6 us
    pallas_call x1, Pallas kernels, body(): pl.pallas_call(lambda *refs: scatter_kernel(n_own, *refs), grid=(early +...  20.4 us
    pallas_call x1, Pallas kernels, body(): pl.pallas_call(lambda *refs: tail_kernel(size, *refs), in_specs=[vmem], o...  14.1 us
    unnamed x9, local copies, waits for them, and re-layouts  2.74 us
    mul x1, other arithmetic, body(): sensitivity = density * (local_sens + tail_offset.reshape(1, -1))  2.54 us

profile of v3, /device:TPU:0, one launch (start us, length us, event | category | flops | bytes accessed | tf_op | source)
XLA Modules:
  0.0 104.0 jit_solution(13184951345413573557)
XLA Ops:
  0.6 0.0 copy-start.2
  0.7 0.7 dynamic-slice_bitcast_fusion.refs_2_
  1.4 0.7 subtract_bitcast_fusion.refs_6_.refs_3_
  2.1 0.7 fusion.1.refs_7_
  2.8 0.8 fusion.4
  3.6 0.0 copy-start
  3.6 0.7 copy-done
  4.3 0.0 copy-start.1
  4.3 0.7 copy-done.1
  5.0 0.0 copy-start.3
  5.0 0.7 copy-done.3
  5.7 60.6 %field.1 = (f32[32,32768]{1,0:T(8,128)S(1)}, f32[32,32768]{1,0:T(8,128)}, f32[16,16,128]{2,1,0:T(8,128)S(1)}, f32[32,1,128]{2,1,0:T(1,128)S(1)}, f32[32,1,128]{2,1,0:T(1,128)S(1)}) custom-call(s32[32,128]{1,0:T(8,128)S(1)} %get-tuple-element.20.refs_0_, f32[32,32768]{1,0:T(8,128)} %refs_1_.1, bf16[64,80]{1,0:T(8,128)(2,1)S(1)} %dynamic-slice_bitcast_fusion.refs_2_, ...), custom_call_target="tpu_custom_call" | custom-call | tf_op jit(solution)/shard_map/field/pallas_call | solution.py:382
  66.3 0.0 copy-done.2
  66.4 20.4 %scatter.1 = (f32[32,32768]{1,0:T(8,128)S(1)}, f32[1,32768]{1,0:T(1,128)S(1)}, f32[32,32768]{1,0:T(8,128)}) custom-call(s32[32,128]{1,0:T(8,128)S(1)} %get-tuple-element.20.refs_0_, f32[32,128]{1,0:T(8,128)S(1)} %get-tuple-element.19.refs_1_, s32[32,128]{1,0:T(8,128)S(1)} %get-tuple-element.22.refs_5_.refs_2_, ...), custom_call_target="tpu_custom_call" | custom-call | tf_op jit(solution)/shard_map/scatter/pallas_call | solution.py:407
  86.7 14.1 %tails.1 = f32[16,16,128]{2,1,0:T(8,128)S(1)} custom-call(f32[16,16,128]{2,1,0:T(8,128)S(1)} %bitcast.42), custom_call_target="tpu_custom_call" | custom-call | tf_op jit(solution)/shard_map/tails/pallas_call | solution.py:423
  100.8 2.5 %add_multiply_fusion = f32[32,32768]{1,0:T(8,128)} fusion(f32[32,32768]{1,0:T(8,128)S(1)} %get-tuple-element.15, f32[32,32768]{1,0:T(8,128)S(1)} %get-tuple-element.16, f32[32768]{0:T(1024)S(1)} %bitcast.40), kind=kLoop, calls=%fused_computation | loop fusion | flops 2097152 | bytes 12713984 | tf_op jit(solution)/shard_map/mul | solution.py:432
  103.4 0.6 copy.14
Async XLA Ops:
  0.6 65.7 %copy-start.2 = (bf16[48,128]{1,0:T(8,128)(2,1)S(1)}, bf16[48,128]{1,0:T(8,128)(2,1)}, u32[]{:S(2)}) copy-start(bf16[48,128]{1,0:T(8,128)(2,1)} %constant.57.clone.refs_5_) | copy-start | bytes 36868
  3.6 0.7 copy-start
  4.3 0.7 copy-start.1
  5.0 0.7 copy-start.3

commit v4 on v3

--- a/solution.py
+++ b/solution.py
@@ -80,10 +80,10 @@
 
 
 def field_kernel(
-    n, n_sky, thickness, row_ref, exc_ref, mat_ref, tri_ref, hi_ref, lo_ref, share_ref, live_ref, obs_ref, inv_ref,
+    n, n_sky, thickness, row_ref, count_ref, exc_ref, mat_ref, hi_ref, lo_ref, frac_ref, obs_hbm, inv_hbm,
     dens_out, pre_out, off_out, res_ref, back_ref,
     last4, first4, before, after, dens_nat, pre_nat, pre_tab, dens_tab, got_rows, base_ref, slope_ref,
-    src, got, summed, col, owned, pull, out_sems, up_send, up_recv, down_send, down_recv, *sems,
+    src, got, summed, col, owned, pull, obs_ref, inv_ref, in_sems, out_sems, up_send, up_recv, down_send, down_recv, *sems,
 ):
     shell = lax.axis_index("shell")
     me = shell * n_sky + lax.axis_index("sky")
@@ -96,6 +96,12 @@
     barrier = pltpu.get_barrier_semaphore()
     others(n_all, me, lambda p: pl.semaphore_signal(
         barrier, inc=1, device_id=where(p), device_id_type=pl.DeviceIdType.MESH))
+    brought = [
+        pltpu.make_async_copy(obs_hbm, obs_ref, in_sems.at[0]),
+        pltpu.make_async_copy(inv_hbm, inv_ref, in_sems.at[1]),
+    ]
+    for copy in brought:
+        copy.start()
     for t in range(tiles):
         at = slice(t * width, (t + 1) * width)
         last4[t] = exc_ref[rows - PASSES :, at]
@@ -138,6 +144,11 @@
             pltpu.make_async_copy(dens_nat.at[t], dens_out.at[:, at], out_sems.at[0, t]),
             pltpu.make_async_copy(pre_nat.at[t], pre_out.at[:, at], out_sems.at[1, t]),
         )
+
+    matrix = mat_ref[jnp.where(shell == 0, 1, 0) + jnp.where(shell == n - 1, 2, 0)]
+    across = lax.broadcasted_iota(jnp.int32, (rows, 2 * rows), 1)
+    across = jnp.where(across >= rows, across - rows, across)
+    tri = (across <= lax.broadcasted_iota(jnp.int32, (rows, 2 * rows), 0)).astype(jnp.bfloat16)
 
     def tile(t, carry):
         pl.when(has_down)(lambda: upward(t).wait_recv())
@@ -145,11 +156,11 @@
         e1, e2 = split2(exc_ref[:, pl.ds(pl.multiple_of(t * width, width), width)])
         h1, h2 = split2(jnp.concatenate([before[t], after[t]], 0))
         stacked = jnp.concatenate([e1, e2, h1, h2], 0).astype(jnp.bfloat16)
-        both = jnp.dot(mat_ref[...], stacked, preferred_element_type=jnp.float32)
+        both = jnp.dot(matrix, stacked, preferred_element_type=jnp.float32)
         dens = jnp.exp(both[:rows] + both[rows:])
         d1, d2 = split2(dens)
         pre = thickness * jnp.dot(
-            tri_ref[...],
+            tri,
             jnp.concatenate([d1, d2], 0).astype(jnp.bfloat16),
             preferred_element_type=jnp.float32,
         )
@@ -169,15 +180,15 @@
     lane = lax.broadcasted_iota(jnp.int32, (LANES, LANES), 1)
     sub = lax.broadcasted_iota(jnp.int32, (LANES, LANES), 0)
 
-    def pick(pair, carry):
-        for k in range(2):
-            o = pair * 2 + k
+    def pick(quad, carry):
+        for k in range(4):
+            o = quad * 4 + k
             for c in range(LANES):
                 at = row_ref[o, c]
                 got_rows[k, c : c + 1, :] = pre_tab[pl.ds(at, 1), :]
                 got_rows[k, LANES + c : LANES + c + 1, :] = dens_tab[pl.ds(at, 1), :]
-        for k in range(2):
-            o = pair * 2 + k
+        for k in range(4):
+            o = quad * 4 + k
             hot = (sub == lo_ref[pl.ds(o, 1), :]).astype(jnp.bfloat16)
             g1, g2 = split2(got_rows[k])
             picked = jnp.dot(
@@ -191,8 +202,8 @@
             slope_ref[pl.ds(o, 1), :] = jnp.sum(jnp.where(sub == lane, d, 0.0), 0, keepdims=True)
         return carry
 
-    pairs = n_all // 2
-    cut = [0, pairs // 2, pairs]
+    quads = n_all // 4
+    cut = [0, quads // 2, quads]
     shell_exchange(
         n, shell, False, src, got, summed, off_out, sems[:4],
         lambda half: lax.fori_loop(cut[half], cut[half + 1], pick, 0),
@@ -202,6 +213,19 @@
     o1, o2 = split2(off_out[...].reshape(groups, LANES))
     table = jnp.concatenate([o1.T, o2.T], 0).astype(jnp.bfloat16)
     tall = lax.broadcasted_iota(jnp.int32, (groups, LANES), 0)
+
+    line = lax.broadcasted_iota(jnp.int32, (1, LANES), 1)
+
+    def move(frm, to, send, recv, peer, slot):
+        return pltpu.make_async_remote_copy(
+            src_ref=frm.at[peer], dst_ref=to.at[slot], send_sem=send.at[peer], recv_sem=recv.at[slot],
+            device_id=where(peer), device_id_type=pl.DeviceIdType.MESH,
+        )
+
+    send3, recv3, send4, recv4 = sems[4:]
+
+    def push(p):
+        pl.when(p != me)(lambda: move(col, owned, send3, recv3, p, me).start())
 
     def chunk(quad, carry):
         for k in range(4):
@@ -211,22 +235,18 @@
             off = jnp.dot(table, hot, preferred_element_type=jnp.float32)
             off = off[:LANES] + off[LANES:]
             off = jnp.sum(jnp.where(sub == lo_ref[at, :], off, 0.0), 0, keepdims=True)
-            value = base_ref[at, :] + off - share_ref[at, :] * thickness * slope_ref[at, :]
-            col[o] = jnp.where(live_ref[at, :] > 0, value, -1.0)
+            value = base_ref[at, :] + off - (1.0 - frac_ref[at, :]) * thickness * slope_ref[at, :]
+            col[o] = jnp.where(line < count_ref[0, o], value, -1.0)
+        for k in range(4):
+            push(quad * 4 + k)
         return carry
 
     lax.fori_loop(0, n_all // 4, chunk, 0)
 
-    def move(frm, to, send, recv, peer, slot):
-        return pltpu.make_async_remote_copy(
-            src_ref=frm.at[peer], dst_ref=to.at[slot], send_sem=send.at[peer], recv_sem=recv.at[slot],
-            device_id=where(peer), device_id_type=pl.DeviceIdType.MESH,
-        )
-
-    send3, recv3, send4, recv4 = sems[4:]
-    others(n_all, me, lambda p: move(col, owned, send3, recv3, p, me).start())
     owned[pl.ds(me, 1)] = col[pl.ds(me, 1)]
     others(n_all, me, lambda p: move(col, owned, send3, recv3, p, p).wait_recv())
+    for copy in brought:
+        copy.wait()
     column = owned[...]
     transmit = jnp.exp(-column)
     inverse = inv_ref[...]
@@ -249,12 +269,12 @@
     lax.fori_loop(0, tiles, drain, 0)
 
 
-GROUP = 8
+GROUP = 16
 CHUNKS = 4
 
 
 def scatter_kernel(
-    n_own, row_ref, rows_ref, lo_ref, share_ref, pull_ref, mat_ref, pre_ref, off_ref,
+    n_own, row_ref, rows_ref, lo_ref, frac_ref, pull_ref, mat_ref, pre_ref, off_ref,
     s_ref, tail_ref, ext_ref, imp_tab, near_tab, upd,
 ):
     step = pl.program_id(0)
@@ -281,13 +301,14 @@
         lane = lax.broadcasted_iota(jnp.int32, (LANES, LANES), 1)
         grouped = sub // GROUP == lane // GROUP
 
-        def chunk(o, carry):
+        for k in range(CHUNKS):
+            o = step * CHUNKS + k
             at = pl.ds(o, 1)
             same = jnp.broadcast_to(rows_ref[at, :], (LANES, LANES))
             same = jnp.logical_and(same == same.T, grouped)
             pull = pull_ref[o]
             a1, a2 = split2(jnp.where(same, pull, 0.0))
-            b1, b2 = split2(jnp.where(same, pull * share_ref[at, :], 0.0))
+            b1, b2 = split2(jnp.where(same, pull * (1.0 - frac_ref[at, :]), 0.0))
             hot = (sub == lo_ref[at, :]).astype(jnp.bfloat16)
             out = lax.dot_general(
                 jnp.concatenate([a1, a2, b1, b2], 0).astype(jnp.bfloat16),
@@ -295,19 +316,18 @@
                 (((1,), (1,)), ((), ())),
                 preferred_element_type=jnp.float32,
             )
-            upd[:LANES] = out[:LANES] + out[LANES : 2 * LANES]
-            upd[LANES:] = out[2 * LANES : 3 * LANES] + out[3 * LANES :]
+            upd[k, :LANES] = out[:LANES] + out[LANES : 2 * LANES]
+            upd[k, LANES:] = out[2 * LANES : 3 * LANES] + out[3 * LANES :]
+        for k in range(CHUNKS):
+            o = step * CHUNKS + k
             for g in range(LANES // GROUP):
                 cs = range(g * GROUP, (g + 1) * GROUP)
                 where = [row_ref[o, c] for c in cs]
-                imps = [imp_tab[pl.ds(w, 1), :] + upd[c : c + 1, :] for w, c in zip(where, cs)]
-                nears = [near_tab[pl.ds(w, 1), :] + upd[LANES + c : LANES + c + 1, :] for w, c in zip(where, cs)]
+                imps = [imp_tab[pl.ds(w, 1), :] + upd[k, c : c + 1, :] for w, c in zip(where, cs)]
+                nears = [near_tab[pl.ds(w, 1), :] + upd[k, LANES + c : LANES + c + 1, :] for w, c in zip(where, cs)]
                 for w, a, b in zip(where, imps, nears):
                     imp_tab[pl.ds(w, 1), :] = a
                     near_tab[pl.ds(w, 1), :] = b
-            return carry
-
-        lax.fori_loop(step * CHUNKS, (step + 1) * CHUNKS, chunk, 0)
 
     def natural(tab):
         parts = []
@@ -332,7 +352,6 @@
 def body(excitation, star_shell, star_pixel, star_fraction, star_count, observed, inverse_error):
     rows, cols = excitation.shape
     size = lax.axis_size("shell")
-    me = lax.axis_index("shell")
     thickness = depth_span / (rows * size)
     n_own = star_shell.shape[1]
     groups = cols // LANES
@@ -342,16 +361,10 @@
     pixel = star_pixel[0]
     hi, lo = pixel // LANES, pixel % LANES
     row = hi * rows + star_shell[0]
-    share = 1.0 - star_fraction[0]
-    live = (jnp.arange(LANES, dtype=jnp.int32)[None, :] < star_count[0][:, None]).astype(jnp.int32)
-
     mats = np.stack([stencil_matrix(rows, a, b) for a, b in ((0, 0), (1, 0), (0, 1), (1, 1))])
     top = mats.astype(bf16)
     rest = (mats - top.astype(np.float32)).astype(bf16)
-    which = (me == 0).astype(jnp.int32) + 2 * (me == size - 1).astype(jnp.int32)
-    mat = lax.dynamic_index_in_dim(jnp.asarray(np.concatenate([top, rest], 1)), which, 0, False)
-    tri = np.tril(np.ones((rows, rows), np.float32))
-    tri2 = jnp.asarray(np.concatenate([tri, tri], 1).astype(bf16))
+    mat = jnp.asarray(np.concatenate([top, rest], 1))
 
     smem = pl.BlockSpec(memory_space=pltpu.SMEM)
     vmem = pl.BlockSpec(memory_space=pltpu.VMEM)
@@ -381,16 +394,16 @@
     tab = pltpu.VMEM((groups * rows, LANES), f32)
     density, prefix, offset, residual, returned = pl.pallas_call(
         lambda *refs: field_kernel(size, n_sky, thickness, *refs),
-        in_specs=[smem] + [vmem] * 9,
+        in_specs=[smem] * 2 + [vmem] * 5 + [hbm] * 2,
         out_specs=[hbm] * 2 + [vmem] * 3,
         out_shape=[grid_shape, grid_shape, blocks, slots, slots],
         scratch_shapes=[edge] * 4 + [nat] * 2 + [tab] * 2
-        + [pltpu.VMEM((2, 2 * LANES, LANES), f32), hold(stars), hold(stars)]
-        + [hold(blocks)] * 3 + [hold(slots)] * 3
-        + [pltpu.SemaphoreType.DMA((2, tiles))] + [dma(tiles)] * 4 + [dma(size)] * 4 + [dma(n_all)] * 4,
+        + [pltpu.VMEM((4, 2 * LANES, LANES), f32), hold(stars), hold(stars)]
+        + [hold(blocks)] * 3 + [hold(slots)] * 5
+        + [dma(2), pltpu.SemaphoreType.DMA((2, tiles))] + [dma(tiles)] * 4 + [dma(size)] * 4 + [dma(n_all)] * 4,
         compiler_params=remote(0),
         name="field",
-    )(row, excitation, mat, tri2, hi, lo, share, live, observed, inverse_error)
+    )(row, star_count, excitation, mat, hi, lo, star_fraction[0], observed, inverse_error)
 
     upper = np.triu(np.ones((rows, rows), np.float32))
     eye = np.eye(rows, dtype=np.float32)
@@ -414,11 +427,11 @@
         scratch_shapes=[
             pltpu.VMEM((groups * rows, LANES), f32),
             pltpu.VMEM((groups * rows, LANES), f32),
-            pltpu.VMEM((2 * LANES, LANES), f32),
+            pltpu.VMEM((CHUNKS, 2 * LANES, LANES), f32),
         ],
         compiler_params=limit,
         name="scatter",
-    )(row, row.astype(f32), lo, share, returned, smat, prefix, offset.reshape(1, -1))
+    )(row, row.astype(f32), lo, star_fraction[0], returned, smat, prefix, offset.reshape(1, -1))
 
     tail_offset = pl.pallas_call(
         lambda *refs: tail_kernel(size, *refs),

time: 105 us -> 98.6 us (0.939)
  Pallas kernels: 95.1 us -> 89.8 us
  other arithmetic: 4.74 us -> 3.3 us
    pallas_call x1, Pallas kernels: 20.4 us -> 17.2 us  [body(): pl.pallas_call(lambda *refs: scatter_kernel(n_own, *refs), grid=(early +...]
    unnamed x9 -> x13, local copies, waits for them, and re-layouts: 2.74 us -> 4.25 us
    pallas_call x1, Pallas kernels: 60.6 us -> 59.4 us  [body(): pl.pallas_call(lambda *refs: field_kernel(size, n_sky, thickness, *refs),...]
where the time goes in v4:
time: 98.6 us; the launch traced here: 98 us
  Pallas kernels  89.8 us (91%)
  local copies, waits for them, and re-layouts  4.25 us (4%)
  other arithmetic  3.3 us (3%)
    pallas_call x1, Pallas kernels, body(): pl.pallas_call(lambda *refs: field_kernel(size, n_sky, thickness, *refs),...  59.4 us
    pallas_call x1, Pallas kernels, body(): pl.pallas_call(lambda *refs: scatter_kernel(n_own, *refs), grid=(early +...  17.2 us
    pallas_call x1, Pallas kernels, body(): pl.pallas_call(lambda *refs: tail_kernel(size, *refs), in_specs=[vmem], o...  13.3 us
    unnamed x13, local copies, waits for them, and re-layouts  4.25 us
    mul x1, other arithmetic, body(): sensitivity = density * (local_sens + tail_offset.reshape(1, -1))  2.54 us

profile of v4, /device:TPU:0, one launch (start us, length us, event | category | flops | bytes accessed | tf_op | source)
XLA Modules:
  0.0 98.0 jit_solution(8287039709854292444)
XLA Ops:
  0.6 0.0 copy-start.4
  0.6 0.8 fusion.3
  1.4 0.0 copy-start
  1.4 0.8 copy-done
  2.2 0.0 copy-start.1
  2.3 0.7 copy-done.1
  3.0 0.0 copy-start.2
  3.0 0.7 copy-done.2
  3.7 0.0 copy-start.3
  3.7 0.7 copy-done.3
  4.4 0.0 copy-start.5
  4.4 0.7 copy-done.5
  5.1 59.4 %field.1 = (f32[32,32768]{1,0:T(8,128)S(1)}, f32[32,32768]{1,0:T(8,128)}, f32[16,16,128]{2,1,0:T(8,128)S(1)}, f32[32,1,128]{2,1,0:T(1,128)S(1)}, f32[32,1,128]{2,1,0:T(1,128)S(1)}) custom-call(s32[32,128]{1,0:T(8,128)S(1)} %get-tuple-element.20.refs_0_, s32[1,32]{1,0:T(1,128)S(1)} %copy-done.5, f32[32,32768]{1,0:T(8,128)} %refs_2_.1, ...), custom_call_target="tpu_custom_call" | custom-call | tf_op jit(solution)/shard_map/field/pallas_call | solution.py:395
  64.4 0.0 copy-done.4
  64.4 17.2 %scatter.1 = (f32[32,32768]{1,0:T(8,128)S(1)}, f32[1,32768]{1,0:T(1,128)S(1)}, f32[32,32768]{1,0:T(8,128)}) custom-call(s32[32,128]{1,0:T(8,128)S(1)} %get-tuple-element.20.refs_0_, f32[32,128]{1,0:T(8,128)S(1)} %get-tuple-element.19.refs_1_, s32[32,128]{1,0:T(8,128)S(1)} %get-tuple-element.22.refs_5_.refs_2_, f32[32,128]{1,0:T(8,128)S(1)} %bitcast.40, ...), custom_call_target="tpu_custom_call" | custom-call | tf_op jit(solution)/shard_map/scatter/pallas_call | solution.py:420
  81.6 13.3 %tails.1 = f32[16,16,128]{2,1,0:T(8,128)S(1)} custom-call(f32[16,16,128]{2,1,0:T(8,128)S(1)} %bitcast.38), custom_call_target="tpu_custom_call" | custom-call | tf_op jit(solution)/shard_map/tails/pallas_call | solution.py:436
  94.9 2.5 %add_multiply_fusion = f32[32,32768]{1,0:T(8,128)} fusion(f32[32,32768]{1,0:T(8,128)S(1)} %get-tuple-element.15, f32[32,32768]{1,0:T(8,128)S(1)} %get-tuple-element.16, f32[32768]{0:T(1024)S(1)} %bitcast.36), kind=kLoop, calls=%fused_computation | loop fusion | flops 2097152 | bytes 12713984 | tf_op jit(solution)/shard_map/mul | solution.py:445
  97.4 0.6 copy.13
Async XLA Ops:
  0.6 63.8 %copy-start.4 = (bf16[48,128]{1,0:T(8,128)(2,1)S(1)}, bf16[48,128]{1,0:T(8,128)(2,1)}, u32[]{:S(2)}) copy-start(bf16[48,128]{1,0:T(8,128)(2,1)} %constant.35.clone.refs_5_) | copy-start | bytes 36868
  1.4 0.8 copy-start
  2.2 0.7 copy-start.1
  3.0 0.7 copy-start.2
  3.7 0.7 copy-start.3
  4.4 0.7 copy-start.5

commit v5 on v4

--- a/solution.py
+++ b/solution.py
@@ -19,21 +19,25 @@
 
 
 def stencil_matrix(rows, first, last):
-    wide = rows + 2 * PASSES
-    valid = np.ones((wide, 1))
-    if first:
-        valid[:PASSES] = 0.0
-    if last:
-        valid[-PASSES:] = 0.0
-    eye = np.eye(wide)
+    pad = 2 * PASSES
+    shape = (rows + 2 * pad, 2 * rows + 4 * PASSES)
+    at = lax.broadcasted_iota(jnp.int32, shape, 0)
+    col = lax.broadcasted_iota(jnp.int32, shape, 1)
+    local = jnp.where(col >= rows, col - rows, col) + pad
+    halo = col - 2 * rows
+    halo = jnp.where(halo >= 2 * PASSES, halo - 2 * PASSES, halo)
+    halo = jnp.where(halo < PASSES, halo + PASSES, halo + rows + PASSES)
+    eye = jnp.where(at == jnp.where(col < 2 * rows, local, halo), 1.0, 0.0)
+    low = jnp.where(first, pad, 0)
+    high = jnp.where(last, rows + pad, rows + 2 * pad)
+    valid = jnp.where(jnp.logical_and(at >= low, at < high), 1.0, 0.0)
+    edge = jnp.zeros((1, shape[1]), jnp.float32)
     out = eye
     for _ in range(PASSES):
-        padded = np.pad(out, ((1, 1), (0, 0)))
-        out = valid * (0.3 * (padded[:-2] + padded[2:]) + 0.35 * out + eye)
-    out = out[PASSES:-PASSES]
-    local = out[:, PASSES:-PASSES]
-    halo = np.concatenate([out[:, :PASSES], out[:, -PASSES:]], 1)
-    return np.concatenate([local, local, halo, halo], 1).astype(np.float32)
+        beside = jnp.concatenate([edge, out[:-1]], 0) + jnp.concatenate([out[1:], edge], 0)
+        out = valid * (0.3 * beside + 0.35 * out + eye)
+    top, rest = split2(out[pad:-pad])
+    return jnp.concatenate([top, rest], 0).astype(jnp.bfloat16)
 
 
 def others(count, me, act):
@@ -80,14 +84,20 @@
 
 
 def field_kernel(
-    n, n_sky, thickness, row_ref, count_ref, exc_ref, mat_ref, hi_ref, lo_ref, frac_ref, obs_hbm, inv_hbm,
+    n, n_sky, thickness, row_ref, hi_ref, lo_ref, exc_hbm, frac_hbm, obs_hbm, inv_hbm,
     dens_out, pre_out, off_out, res_ref, back_ref,
     last4, first4, before, after, dens_nat, pre_nat, pre_tab, dens_tab, got_rows, base_ref, slope_ref,
-    src, got, summed, col, owned, pull, obs_ref, inv_ref, in_sems, out_sems, up_send, up_recv, down_send, down_recv, *sems,
+    src, got, summed, col, owned, pull, exc_ref, frac_ref, obs_ref, inv_ref, in_sems, out_sems, up_send, up_recv, down_send, down_recv, *sems,
 ):
     shell = lax.axis_index("shell")
     me = shell * n_sky + lax.axis_index("sky")
     n_all = n * n_sky
+    pairs = (
+        (exc_hbm, exc_ref), (frac_hbm, frac_ref), (obs_hbm, obs_ref), (inv_hbm, inv_ref),
+    )
+    brought = [pltpu.make_async_copy(a, b, in_sems.at[i]) for i, (a, b) in enumerate(pairs)]
+    for copy in brought:
+        copy.start()
     rows, cols = exc_ref.shape
     tiles, _, width = last4.shape
     blocks = width // LANES
@@ -96,12 +106,8 @@
     barrier = pltpu.get_barrier_semaphore()
     others(n_all, me, lambda p: pl.semaphore_signal(
         barrier, inc=1, device_id=where(p), device_id_type=pl.DeviceIdType.MESH))
-    brought = [
-        pltpu.make_async_copy(obs_hbm, obs_ref, in_sems.at[0]),
-        pltpu.make_async_copy(inv_hbm, inv_ref, in_sems.at[1]),
-    ]
-    for copy in brought:
-        copy.start()
+    matrix = stencil_matrix(rows, shell == 0, shell == n - 1)
+    brought[0].wait()
     for t in range(tiles):
         at = slice(t * width, (t + 1) * width)
         last4[t] = exc_ref[rows - PASSES :, at]
@@ -145,7 +151,8 @@
             pltpu.make_async_copy(pre_nat.at[t], pre_out.at[:, at], out_sems.at[1, t]),
         )
 
-    matrix = mat_ref[jnp.where(shell == 0, 1, 0) + jnp.where(shell == n - 1, 2, 0)]
+    for copy in brought[1:]:
+        copy.wait()
     across = lax.broadcasted_iota(jnp.int32, (rows, 2 * rows), 1)
     across = jnp.where(across >= rows, across - rows, across)
     tri = (across <= lax.broadcasted_iota(jnp.int32, (rows, 2 * rows), 0)).astype(jnp.bfloat16)
@@ -214,8 +221,6 @@
     table = jnp.concatenate([o1.T, o2.T], 0).astype(jnp.bfloat16)
     tall = lax.broadcasted_iota(jnp.int32, (groups, LANES), 0)
 
-    line = lax.broadcasted_iota(jnp.int32, (1, LANES), 1)
-
     def move(frm, to, send, recv, peer, slot):
         return pltpu.make_async_remote_copy(
             src_ref=frm.at[peer], dst_ref=to.at[slot], send_sem=send.at[peer], recv_sem=recv.at[slot],
@@ -236,7 +241,7 @@
             off = off[:LANES] + off[LANES:]
             off = jnp.sum(jnp.where(sub == lo_ref[at, :], off, 0.0), 0, keepdims=True)
             value = base_ref[at, :] + off - (1.0 - frac_ref[at, :]) * thickness * slope_ref[at, :]
-            col[o] = jnp.where(line < count_ref[0, o], value, -1.0)
+            col[o] = jnp.where(hi_ref[at, :] < groups, value, -1.0)
         for k in range(4):
             push(quad * 4 + k)
         return carry
@@ -245,8 +250,6 @@
 
     owned[pl.ds(me, 1)] = col[pl.ds(me, 1)]
     others(n_all, me, lambda p: move(col, owned, send3, recv3, p, p).wait_recv())
-    for copy in brought:
-        copy.wait()
     column = owned[...]
     transmit = jnp.exp(-column)
     inverse = inv_ref[...]
@@ -361,10 +364,8 @@
     pixel = star_pixel[0]
     hi, lo = pixel // LANES, pixel % LANES
     row = hi * rows + star_shell[0]
-    mats = np.stack([stencil_matrix(rows, a, b) for a, b in ((0, 0), (1, 0), (0, 1), (1, 1))])
-    top = mats.astype(bf16)
-    rest = (mats - top.astype(np.float32)).astype(bf16)
-    mat = jnp.asarray(np.concatenate([top, rest], 1))
+    live = jnp.arange(LANES, dtype=jnp.int32)[None, :] < star_count[0][:, None]
+    hi = jnp.where(live, hi, groups)
 
     smem = pl.BlockSpec(memory_space=pltpu.SMEM)
     vmem = pl.BlockSpec(memory_space=pltpu.VMEM)
@@ -394,16 +395,17 @@
     tab = pltpu.VMEM((groups * rows, LANES), f32)
     density, prefix, offset, residual, returned = pl.pallas_call(
         lambda *refs: field_kernel(size, n_sky, thickness, *refs),
-        in_specs=[smem] * 2 + [vmem] * 5 + [hbm] * 2,
+        in_specs=[smem, vmem, vmem] + [hbm] * 4,
         out_specs=[hbm] * 2 + [vmem] * 3,
         out_shape=[grid_shape, grid_shape, blocks, slots, slots],
         scratch_shapes=[edge] * 4 + [nat] * 2 + [tab] * 2
         + [pltpu.VMEM((4, 2 * LANES, LANES), f32), hold(stars), hold(stars)]
-        + [hold(blocks)] * 3 + [hold(slots)] * 5
-        + [dma(2), pltpu.SemaphoreType.DMA((2, tiles))] + [dma(tiles)] * 4 + [dma(size)] * 4 + [dma(n_all)] * 4,
+        + [hold(blocks)] * 3 + [hold(slots)] * 3
+        + [pltpu.VMEM((rows, cols), f32), hold(stars), hold(slots), hold(slots)]
+        + [dma(4), pltpu.SemaphoreType.DMA((2, tiles))] + [dma(tiles)] * 4 + [dma(size)] * 4 + [dma(n_all)] * 4,
         compiler_params=remote(0),
         name="field",
-    )(row, star_count, excitation, mat, hi, lo, star_fraction[0], observed, inverse_error)
+    )(row, hi, lo, excitation, star_fraction[0], observed, inverse_error)
 
     upper = np.triu(np.ones((rows, rows), np.float32))
     eye = np.eye(rows, dtype=np.float32)

time: 98.6 us -> 95.8 us (0.972)
  local copies, waits for them, and re-layouts: 4.25 us -> 2.76 us
  Pallas kernels: 89.8 us -> 88.5 us
    unnamed x13 -> x9, local copies, waits for them, and re-layouts: 4.25 us -> 2.76 us
    pallas_call x1, Pallas kernels: 59.4 us -> 58.1 us  [body(): pl.pallas_call(lambda *refs: field_kernel(size, n_sky, thickness, *refs),...]
where the time goes in v5:
time: 95.8 us; the launch traced here: 95.3 us
  Pallas kernels  88.5 us (92%)
  other arithmetic  3.37 us (4%)
  local copies, waits for them, and re-layouts  2.76 us (3%)
    pallas_call x1, Pallas kernels, body(): pl.pallas_call(lambda *refs: field_kernel(size, n_sky, thickness, *refs),...  58.1 us
    pallas_call x1, Pallas kernels, body(): pl.pallas_call(lambda *refs: scatter_kernel(n_own, *refs), grid=(early +...  17.2 us
    pallas_call x1, Pallas kernels, body(): pl.pallas_call(lambda *refs: tail_kernel(size, *refs), in_specs=[vmem], o...  13.2 us
    unnamed x9, local copies, waits for them, and re-layouts  2.76 us
    mul x1, other arithmetic, body(): sensitivity = density * (local_sens + tail_offset.reshape(1, -1))  2.54 us

profile of v5, /device:TPU:0, one launch (start us, length us, event | category | flops | bytes accessed | tf_op | source)
XLA Modules:
  0.0 95.3 jit_solution(4970422087532538720)
XLA Ops:
  0.6 0.0 copy-start.3
  0.6 0.8 fusion.1
  1.5 0.0 copy-start
  1.5 0.7 copy-done
  2.2 0.0 copy-start.1
  2.2 0.7 copy-done.1
  2.9 0.0 copy-start.2
  2.9 0.7 copy-done.2
  3.6 58.1 %field.1 = (f32[32,32768]{1,0:T(8,128)S(1)}, f32[32,32768]{1,0:T(8,128)}, f32[16,16,128]{2,1,0:T(8,128)S(1)}, f32[32,1,128]{2,1,0:T(1,128)S(1)}, f32[32,1,128]{2,1,0:T(1,128)S(1)}) custom-call(s32[32,128]{1,0:T(8,128)S(1)} %get-tuple-element.24.refs_0_, s32[32,128]{1,0:T(8,128)S(1)} %get-tuple-element.21.refs_1_, s32[32,128]{1,0:T(8,128)S(1)} %get-tuple-element.22.refs_2_, ...), custom_call_target="tpu_custom_call" | custom-call | tf_op jit(solution)/shard_map/field/pallas_call | solution.py:396
  61.7 0.0 copy-done.3
  61.7 17.2 %scatter.1 = (f32[32,32768]{1,0:T(8,128)S(1)}, f32[1,32768]{1,0:T(1,128)S(1)}, f32[32,32768]{1,0:T(8,128)}) custom-call(s32[32,128]{1,0:T(8,128)S(1)} %get-tuple-element.24.refs_0_, f32[32,128]{1,0:T(8,128)S(1)} %get-tuple-element.23.refs_1_, s32[32,128]{1,0:T(8,128)S(1)} %get-tuple-element.22.refs_2_, f32[32,128]{1,0:T(8,128)S(1)} %bitcast.43, ...), custom_call_target="tpu_custom_call" | custom-call | tf_op jit(solution)/shard_map/scatter/pallas_call | solution.py:422
  78.9 13.2 %tails.1 = f32[16,16,128]{2,1,0:T(8,128)S(1)} custom-call(f32[16,16,128]{2,1,0:T(8,128)S(1)} %bitcast.41), custom_call_target="tpu_custom_call" | custom-call | tf_op jit(solution)/shard_map/tails/pallas_call | solution.py:438
  92.2 2.5 %add_multiply_fusion = f32[32,32768]{1,0:T(8,128)} fusion(f32[32,32768]{1,0:T(8,128)S(1)} %get-tuple-element.15, f32[32,32768]{1,0:T(8,128)S(1)} %get-tuple-element.16, f32[32768]{0:T(1024)S(1)} %bitcast.39), kind=kLoop, calls=%fused_computation | loop fusion | flops 2097152 | bytes 12713984 | tf_op jit(solution)/shard_map/mul | solution.py:447
  94.7 0.6 copy.12
Async XLA Ops:
  0.6 61.1 %copy-start.3 = (bf16[48,128]{1,0:T(8,128)(2,1)S(1)}, bf16[48,128]{1,0:T(8,128)(2,1)}, u32[]{:S(2)}) copy-start(bf16[48,128]{1,0:T(8,128)(2,1)} %constant.34.clone.refs_5_) | copy-start | bytes 36868
  1.5 0.7 copy-start
  2.2 0.7 copy-start.1
  2.9 0.7 copy-start.2

commit v6 on v5

--- a/solution.py
+++ b/solution.py
@@ -272,7 +272,7 @@
     lax.fori_loop(0, tiles, drain, 0)
 
 
-GROUP = 16
+GROUP = 32
 CHUNKS = 4
 
 

time: 95.8 us -> 96.9 us (1.011)
  Pallas kernels: 88.5 us -> 89.5 us
    pallas_call x1, Pallas kernels: 17.2 us -> 18.2 us  [body(): pl.pallas_call(lambda *refs: scatter_kernel(n_own, *refs), grid=(early +...]
where the time goes in v6:
time: 96.9 us; the launch traced here: 96.3 us
  Pallas kernels  89.5 us (92%)
  other arithmetic  3.37 us (3%)
  local copies, waits for them, and re-layouts  2.76 us (3%)
    pallas_call x1, Pallas kernels, body(): pl.pallas_call(lambda *refs: field_kernel(size, n_sky, thickness, *refs),...  58.1 us
    pallas_call x1, Pallas kernels, body(): pl.pallas_call(lambda *refs: scatter_kernel(n_own, *refs), grid=(early +...  18.2 us
    pallas_call x1, Pallas kernels, body(): pl.pallas_call(lambda *refs: tail_kernel(size, *refs), in_specs=[vmem], o...  13.3 us
    unnamed x9, local copies, waits for them, and re-layouts  2.76 us
    mul x1, other arithmetic, body(): sensitivity = density * (local_sens + tail_offset.reshape(1, -1))  2.54 us

profile of v6, /device:TPU:0, one launch (start us, length us, event | category | flops | bytes accessed | tf_op | source)
XLA Modules:
  0.0 96.3 jit_solution(14834688840936850299)
XLA Ops:
  0.6 0.0 copy-start.3
  0.6 0.8 fusion.1
  1.5 0.0 copy-start
  1.5 0.7 copy-done
  2.2 0.0 copy-start.1
  2.2 0.7 copy-done.1
  2.9 0.0 copy-start.2
  2.9 0.7 copy-done.2
  3.6 58.1 %field.1 = (f32[32,32768]{1,0:T(8,128)S(1)}, f32[32,32768]{1,0:T(8,128)}, f32[16,16,128]{2,1,0:T(8,128)S(1)}, f32[32,1,128]{2,1,0:T(1,128)S(1)}, f32[32,1,128]{2,1,0:T(1,128)S(1)}) custom-call(s32[32,128]{1,0:T(8,128)S(1)} %get-tuple-element.24.refs_0_, s32[32,128]{1,0:T(8,128)S(1)} %get-tuple-element.21.refs_1_, s32[32,128]{1,0:T(8,128)S(1)} %get-tuple-element.22.refs_2_, ...), custom_call_target="tpu_custom_call" | custom-call | tf_op jit(solution)/shard_map/field/pallas_call | solution.py:396
  61.7 0.0 copy-done.3
  61.7 18.2 %scatter.1 = (f32[32,32768]{1,0:T(8,128)S(1)}, f32[1,32768]{1,0:T(1,128)S(1)}, f32[32,32768]{1,0:T(8,128)}) custom-call(s32[32,128]{1,0:T(8,128)S(1)} %get-tuple-element.24.refs_0_, f32[32,128]{1,0:T(8,128)S(1)} %get-tuple-element.23.refs_1_, s32[32,128]{1,0:T(8,128)S(1)} %get-tuple-element.22.refs_2_, f32[32,128]{1,0:T(8,128)S(1)} %bitcast.43, ...), custom_call_target="tpu_custom_call" | custom-call | tf_op jit(solution)/shard_map/scatter/pallas_call | solution.py:422
  79.9 13.3 %tails.1 = f32[16,16,128]{2,1,0:T(8,128)S(1)} custom-call(f32[16,16,128]{2,1,0:T(8,128)S(1)} %bitcast.41), custom_call_target="tpu_custom_call" | custom-call | tf_op jit(solution)/shard_map/tails/pallas_call | solution.py:438
  93.2 2.5 %add_multiply_fusion = f32[32,32768]{1,0:T(8,128)} fusion(f32[32,32768]{1,0:T(8,128)S(1)} %get-tuple-element.15, f32[32,32768]{1,0:T(8,128)S(1)} %get-tuple-element.16, f32[32768]{0:T(1024)S(1)} %bitcast.39), kind=kLoop, calls=%fused_computation | loop fusion | flops 2097152 | bytes 12713984 | tf_op jit(solution)/shard_map/mul | solution.py:447
  95.7 0.6 copy.12
Async XLA Ops:
  0.6 61.1 %copy-start.3 = (bf16[48,128]{1,0:T(8,128)(2,1)S(1)}, bf16[48,128]{1,0:T(8,128)(2,1)}, u32[]{:S(2)}) copy-start(bf16[48,128]{1,0:T(8,128)(2,1)} %constant.34.clone.refs_5_) | copy-start | bytes 36868
  1.5 0.7 copy-start
  2.2 0.7 copy-start.1
  2.9 0.7 copy-start.2
